TPU v7x, 512 devices: a whole 4x8x8 slice. The times are simulated.
512 devices in a mesh: ctx: 64 (over z, y_lo, x), head: 8 (over y_hi, core).
Axes of the slice: x: 4, y: 8 (y_hi: 4, y_lo: 2; y = y_hi * 2 + y_lo), z: 8, core: 2. Of those that a mesh axis runs over, the one named last changes fastest.
Arguments:
- queries: bfloat16 [12288, 32, 128], P(('ctx', 'head')), may hold values from -10 to 10
- keys_values: bfloat16 [12288, 8, 256], P(('ctx', 'head')), may hold values from -10 to 10
- span_order: int32 [128], replicated, may hold values from 0 to 127, each once
Outputs:
- attended: bfloat16 [12288, 32, 128], P(('ctx', 'head'))
Inputs may be any that keep to these rules, and one draw needn't show every extreme that they name: A permutation: layout span c holds the sequence positions span_order[c] * 96 to span_order[c] * 96 + 95 in order.
All inputs are finite; a program needn't handle non-finite values.
Results may differ from a plain program's by a relative error of at most 0.005.
Values may be sent and summed in bfloat16 or wider, within the bound.
No kernel may reach another device: no remote copies, remote signals or barrier semaphores. Data moves between devices by JAX's collectives and lax.ppermute only.
A program may use at most 64 MiB of HBM per device.

v0:
```python
import math

import jax
import jax.numpy as jnp
from jax import lax
from jax.sharding import PartitionSpec as P

HEADS = 32
KV_HEADS = 8
HEAD_DIM = 128
SPAN = 96


def place_rows(start, row_count, span_order):
    rows = start + jnp.arange(row_count, dtype=jnp.int32)
    span_index = rows // SPAN
    slots = jnp.arange(span_order.shape[0], dtype=jnp.int32)
    picked = jnp.sum(
        jnp.where(span_index[:, None] == slots[None, :], span_order[None, :], 0), axis=1
    )
    return picked * SPAN + rows % SPAN


def absorb_block(carry, block_rows, start, grouped_q, query_pos, span_order):
    scale = 1.0 / math.sqrt(HEAD_DIM)
    key_pos = place_rows(start, block_rows.shape[0], span_order)
    allowed = key_pos[None, :] <= query_pos[:, None]
    running_max, denominator, accumulated = carry
    key_part = block_rows[:, :, :HEAD_DIM]
    value_part = block_rows[:, :, HEAD_DIM:]
    scores = (
        jnp.einsum("tkgd,skd->kgts", grouped_q, key_part, preferred_element_type=jnp.float32)
        * scale
    )
    masked_scores = jnp.where(allowed[None, None], scores, -1e30)
    new_max = jnp.maximum(running_max, jnp.max(masked_scores, axis=-1))
    weights = jnp.where(allowed[None, None], jnp.exp(scores - new_max[..., None]), 0.0)
    rescale = jnp.exp(running_max - new_max)
    denominator = denominator * rescale + jnp.sum(weights, axis=-1)
    product = jnp.einsum(
        "kgts,skd->tkgd",
        weights.astype(jnp.bfloat16),
        value_part,
        preferred_element_type=jnp.float32,
    )
    accumulated = accumulated * jnp.transpose(rescale, (2, 0, 1))[..., None] + product
    return (new_max, denominator, accumulated)


def absorb(carry, piece, start, grouped_q, query_pos, span_order):
    row_count = piece.shape[0]

    def advance(block_index, inner):
        block_rows = lax.dynamic_slice_in_dim(piece, block_index * 512, 512, 0)
        return absorb_block(
            inner, block_rows, start + block_index * 512, grouped_q, query_pos, span_order
        )

    return lax.fori_loop(0, row_count // 512, advance, carry)


def shards(queries, keys_values, span_order):
    mine_q, mine_kv = (
        lax.all_to_all(queries, "head", split_axis=1, concat_axis=0, tiled=True),
        lax.all_to_all(keys_values, "head", split_axis=1, concat_axis=0, tiled=True),
    )
    tok_rows = mine_q.shape[0]
    local_kv = mine_kv.shape[1]
    group = HEADS // KV_HEADS
    grouped_q = mine_q.reshape(tok_rows, local_kv, group, HEAD_DIM)
    query_pos = place_rows(lax.axis_index("ctx") * tok_rows, tok_rows, span_order)
    initial = (
        jnp.full((local_kv, group, tok_rows), -1e30, jnp.float32),
        jnp.zeros((local_kv, group, tok_rows), jnp.float32),
        jnp.zeros((tok_rows, local_kv, group, HEAD_DIM), jnp.float32),
    )
    gathered = lax.all_gather(mine_kv, "ctx", axis=0, tiled=True)
    final_state = absorb(initial, gathered, 0, grouped_q, query_pos, span_order)
    running_max, denominator, accumulated = final_state
    output = accumulated / jnp.transpose(denominator, (2, 0, 1))[..., None]
    output = output.reshape(tok_rows, local_kv * group, HEAD_DIM).astype(jnp.bfloat16)
    return lax.all_to_all(output, "head", split_axis=0, concat_axis=1, tiled=True)


def solution(mesh):
    placed = (P(("ctx", "head"), None, None), P(("ctx", "head"), None, None), P())
    return jax.shard_map(
        shards,
        mesh=mesh,
        in_specs=placed,
        out_specs=P(("ctx", "head"), None, None),
        check_vma=False,
    )
```

profile of v0, /device:TPU:1, one launch (start us, length us, event | category | flops | bytes accessed | tf_op | source)
XLA Modules:
  0.0 453.7 jit_solution(5033864713546777734)
XLA Ops:
  7.5 17.6 %all_to_all.51 = bf16[24,8,256]{2,0,1:T(8,128)(2,1)} all-to-all(bf16[24,8,256]{2,0,1:T(8,128)(2,1)S(1)} %copy.13), channel_id=1, replica_groups=mesh['ctx'=64,'head'=8] {'head'}, dimensions={1} | all-to-all | bytes 196608 | tf_op jit(solution)/shard_map/all_to_all | solution.py:65
  25.0 1.7 copy.14
  26.7 4.4 all-to-all-start.1
  32.0 8.5 %all-to-all-done.1 = bf16[24,32,128]{2,0,1:T(8,128)(2,1)S(1)} async-done(((bf16[24,32,128]{2,0,1:T(8,128)(2,1)}), bf16[24,32,128]{2,0,1:T(8,128)(2,1)S(1)}, u32[]{:S(2)}, u32[]{:S(2)}) %all-to-all-start.1) | async-done | bytes 196640 | tf_op jit(solution)/shard_map/all_to_all | solution.py:64
  40.5 253.9 %all-gather.2.cloned.1.call-done = bf16[12288,1,256]{2,0,1:T(8,128)(2,1)} async-done(((bf16[192,1,256]{2,0,1:T(8,128)(2,1)}), bf16[12288,1,256]{2,0,1:T(8,128)(2,1)}) %all-gather.2.cloned.1.call-update) | async-done | bytes 6291472 | tf_op jit(solution)/shard_map/all_gather | solution.py:77
  294.4 94.4 %while.20 = (s32[]{:T(128)}, f32[1,4,192]{2,1,0:T(4,128)S(1)}, f32[1,4,192]{2,1,0:T(4,128)S(1)}, f32[192,1,4,128]{3,0,2,1:T(8,128)S(1)}, s32[128]{0:T(128)S(1)},...) while((s32[]{:T(128)}, f32[1,4,192]{2,1,0:T(4,128)S(1)}, ...), condition=%wide.region_5.6_spmd.clone, body=%wide.region_1.5_spmd.clone.sunk | while | flops 205468672 | bytes 6419927 | solution.py:59
  294.8 1.4 fusion.35
  296.3 1.5 fusion.38
  300.2 1.5 fusion.38
  304.1 1.5 fusion.38
  308.1 1.5 fusion.38
  312.0 1.5 fusion.38
  315.9 1.5 fusion.38
  319.9 1.5 fusion.38
  323.8 1.5 fusion.38
  327.8 1.5 fusion.38
  331.7 1.5 fusion.38
  335.6 1.5 fusion.38
  339.6 1.5 fusion.38
  343.5 1.5 fusion.38
  347.4 1.5 fusion.38
  351.4 1.5 fusion.38
  355.3 1.5 fusion.38
  359.2 1.5 fusion.38
  363.2 1.5 fusion.38
  367.1 1.5 fusion.38
  371.1 1.5 fusion.38
  375.0 1.5 fusion.38
  378.9 1.5 fusion.38
  382.9 1.5 fusion.38
  386.8 1.5 fusion.38
  389.4 56.8 %all_to_all.52 = bf16[192,4,128]{2,1,0:T(4,128)(2,1)S(1)} all-to-all(bf16[192,4,128]{2,1,0:T(4,128)(2,1)S(1)} %fusion.23), channel_id=1, replica_groups=mesh['ctx'=64,'head'=8] {'head'}, dimensions={0} | all-to-all | bytes 393216 | tf_op jit(solution)/shard_map/all_to_all | solution.py:82
  (230 shorter events, 59.1 us)
Async XLA Ops:
  6.5 287.9 %copy-start = (s32[128]{0:T(128)S(1)}, s32[128]{0:T(128)}, u32[]{:S(2)}) copy-start(s32[128]{0:T(128)} %param.7) | copy-start | bytes 1540
  6.5 287.9 %all-gather.2.cloned.1.call-start = ((), (), s32[]{:S(2)}) async-start(), calls=%async_computation.3 | async-start | bytes 6389760 | tf_op jit(solution)/shard_map/all_gather | solution.py:77
  26.7 13.7 %all-to-all-start.1 = ((bf16[24,32,128]{2,0,1:T(8,128)(2,1)}), bf16[24,32,128]{2,0,1:T(8,128)(2,1)S(1)}, u32[]{:S(2)}, u32[]{:S(2)}) async-start(bf16[24,32,128]{2,0,1:T(8,128)(2,1)} %copy.14), calls=%async_computation.1 | async-start | bytes 393216 | tf_op jit(solution)/shard_map/all_to_all | solution.py:64
Sparse Core Ops, SparseCore 0:
  25.2 269.2 all-gather.1
where the time goes:
time: 455 us; the launch traced here: 454 us
  waiting for transfers between devices  262 us (58%)
  blocking collectives  74.3 us (16%)
  matrix products  69.4 us (15%)
  other arithmetic  24.8 us (5%)
  between operations  13.5 us (3%)
    all_gather x1, waiting for transfers between devices, shards(): gathered = lax.all_gather(mine_kv, 'ctx', axis=0, tiled=True)  254 us
    all_to_all x1, blocking collectives, shards(): lax.all_to_all(output, 'head', split_axis=0, concat_axis=1, tiled=True)  56.8 us
    dot_general x24, matrix products, absorb_block(): jnp.einsum('kgts,skd->tkgd', weights.astype(jnp.bfloat16), value_part, pr...  35.5 us
    dot_general x24, matrix products, absorb_block(): jnp.einsum('tkgd,skd->kgts', grouped_q, key_part, preferred_element_type=...  33.8 us
    all_to_all x1, blocking collectives, shards(): lax.all_to_all(keys_values, 'head', split_axis=1, concat_axis=0, tiled=True)  17.6 us
    reduce_sum x24, other arithmetic, absorb_block(): denominator = denominator * rescale + jnp.sum(weights, axis=-1)  13.6 us
  transfers between devices with their start and end apart: 2, of which 2 were waited for; matrix products, arithmetic and copies ran while one was open for 1% of the time, Pallas kernels for 0%

commit v1 on v0

v1 whole, which is shorter than its diff:
```python
import functools
import math

import jax
import jax.numpy as jnp
from jax import lax
from jax.experimental import pallas as pl
from jax.experimental.pallas import tpu as pltpu
from jax.sharding import Mesh, PartitionSpec as P

HEADS = 32
KV_HEADS = 8
GROUP = HEADS // KV_HEADS
HEAD_DIM = 128
HALF = 48
Q_UNITS = 16
K_UNITS = 64
PAIRS = Q_UNITS // 2
CHUNK_UNITS = 8
CHUNK = CHUNK_UNITS * HALF
Q_COLS = GROUP * HEAD_DIM
EXPONENT = math.log2(math.e) / math.sqrt(HEAD_DIM)
LOWEST = -1e30

AXES = ("zh", "zl", "yl", "x", "yh", "core")
SIZES = (4, 2, 2, 4, 4, 2)
HEAD_AXES = ("zl", "yl", "core")
KEY_AXES = ("zh", "yh")


def plan(span_order):
    order = span_order.reshape(4, 2, 2, 4, 2)
    x_is = lax.axis_index("x") == jnp.arange(4)
    zh_is = lax.axis_index("zh") == jnp.arange(4)
    yh = lax.axis_index("yh")
    s_is = (yh // 2) == jnp.arange(2)
    keys = jnp.sum(jnp.where(x_is[:, None], order, 0), axis=3)
    keys = keys[..., None] * 2 + jnp.arange(2)
    keys = jnp.transpose(keys, (0, 3, 4, 1, 2)).reshape(K_UNITS)
    mine = jnp.sum(jnp.where(zh_is[:, None, None, None, None], order, 0), axis=0)
    mine = jnp.sum(jnp.where(s_is, mine, 0), axis=-1)
    queries = jnp.transpose(mine, (2, 0, 1)).reshape(Q_UNITS) * 2 + yh % 2

    def ranked(values):
        n = values.shape[0]
        rank = jnp.sum((values[None, :] < values[:, None]).astype(jnp.int32), axis=1)
        hit = rank[:, None] == jnp.arange(n)[None, :]
        index = jnp.sum(jnp.where(hit, jnp.arange(n)[:, None], 0), axis=0)
        return index, jnp.sum(jnp.where(hit, values[:, None], 0), axis=0)

    k_index, k_sorted = ranked(keys)
    q_index, q_sorted = ranked(queries)
    below = jnp.sum((k_sorted[None, :] < q_sorted[:, None]).astype(jnp.int32), axis=1)
    upto = jnp.sum((k_sorted[None, :] <= q_sorted[:, None]).astype(jnp.int32), axis=1)
    scalars = jnp.concatenate([k_index, q_index, q_sorted, below, upto]).astype(jnp.int32)
    columns = k_sorted[:, None] * HALF + jnp.arange(HALF)[None, :]
    return scalars, columns.reshape(1, K_UNITS * HALF).astype(jnp.int32)


def attend_kernel(scalars, columns, q_ref, kv_ref, out_ref, keys, values, q_pair, top, total):
    k_index, q_index, q_sorted, below, upto = 0, 64, 80, 96, 112
    rows = GROUP * HALF

    values[:, HEAD_DIM:] = jnp.ones((K_UNITS * HALF, HEAD_DIM), jnp.bfloat16)

    def place(unit, _):
        source = pl.multiple_of(scalars[k_index + unit] * HALF, HALF)
        target = pl.multiple_of(unit * HALF, HALF)
        block = kv_ref[pl.ds(source, HALF), :]
        keys[pl.ds(target, HALF), :] = block[:, :HEAD_DIM]
        values[pl.ds(target, HALF), :HEAD_DIM] = block[:, HEAD_DIM:]
        return 0

    lax.fori_loop(0, K_UNITS, place, 0)

    def run_pair(pair, _):
        for side in range(2):
            source = pl.multiple_of(scalars[q_index + 2 * pair + side] * HALF, HALF)
            for g in range(GROUP):
                q_pair[side, g * HALF : (g + 1) * HALF, :] = q_ref[
                    pl.ds(source, HALF), g * HEAD_DIM : (g + 1) * HEAD_DIM
                ]
        top[...] = jnp.full(top.shape, LOWEST, jnp.float32)
        total[...] = jnp.zeros(total.shape, jnp.float32)

        def step(chunk, masked):
            start = pl.multiple_of(chunk * CHUNK, CHUNK)
            key_block = keys[pl.ds(start, CHUNK), :]
            value_block = values[pl.ds(start, CHUNK), :]
            for side in range(2):
                scores = lax.dot_general(
                    q_pair[side],
                    key_block,
                    (((1,), (1,)), ((), ())),
                    preferred_element_type=jnp.float32,
                )
                if masked:
                    row = lax.broadcasted_iota(jnp.int32, (rows, CHUNK), 0) % HALF
                    row = row + scalars[q_sorted + 2 * pair + side] * HALF
                    allowed = columns[:, pl.ds(start, CHUNK)] <= row
                    scores = jnp.where(allowed, scores, LOWEST)
                old_top = top[side]
                new_top = jnp.maximum(old_top, jnp.max(scores, axis=1, keepdims=True))
                weights = jnp.exp2((scores - new_top[:, :1]) * EXPONENT)
                if masked:
                    weights = jnp.where(allowed, weights, 0.0)
                rescale = jnp.exp2((old_top - new_top) * EXPONENT)
                product = jnp.dot(
                    weights.astype(jnp.bfloat16),
                    value_block,
                    preferred_element_type=jnp.float32,
                )
                top[side] = new_top
                total[side] = total[side] * jnp.concatenate([rescale, rescale], axis=1) + product

        free_chunks = scalars[below + 2 * pair] // CHUNK_UNITS
        all_chunks = (scalars[upto + 2 * pair + 1] + CHUNK_UNITS - 1) // CHUNK_UNITS

        def free_step(chunk, _):
            step(chunk, False)
            return 0

        def masked_step(chunk, _):
            step(chunk, True)
            return 0

        lax.fori_loop(0, free_chunks, free_step, 0)
        lax.fori_loop(free_chunks, all_chunks, masked_step, 0)

        lane = lax.broadcasted_iota(jnp.int32, (HALF, HEAD_DIM), 1)
        for side in range(2):
            target = pl.multiple_of(scalars[q_index + 2 * pair + side] * HALF, HALF)
            stats = jnp.zeros((HALF, HEAD_DIM), jnp.float32)
            for g in range(GROUP):
                part = slice(g * HALF, (g + 1) * HALF)
                weight_sum = total[side, part, HEAD_DIM:]
                some = weight_sum > 0.0
                safe = jnp.where(some, weight_sum, 1.0)
                out_ref[pl.ds(target, HALF), g * HEAD_DIM : (g + 1) * HEAD_DIM] = (
                    total[side, part, :HEAD_DIM] / safe
                ).astype(jnp.bfloat16)
                level = jnp.where(some, top[side, part, :] * EXPONENT + jnp.log2(safe), LOWEST)
                high = level.astype(jnp.bfloat16).astype(jnp.float32)
                rest = level - high
                middle = rest.astype(jnp.bfloat16).astype(jnp.float32)
                low = rest - middle
                stats = jnp.where(lane == 3 * g, high, stats)
                stats = jnp.where(lane == 3 * g + 1, middle, stats)
                stats = jnp.where(lane == 3 * g + 2, low, stats)
            out_ref[pl.ds(target, HALF), Q_COLS:] = stats.astype(jnp.bfloat16)
        return 0

    lax.fori_loop(0, PAIRS, run_pair, 0)


def attend(scalars, columns, queries, keys_values):
    vmem = pl.BlockSpec(memory_space=pltpu.VMEM)
    return pl.pallas_call(
        attend_kernel,
        out_shape=jax.ShapeDtypeStruct((Q_UNITS * HALF, Q_COLS + HEAD_DIM), jnp.bfloat16),
        in_specs=[pl.BlockSpec(memory_space=pltpu.SMEM), vmem, vmem, vmem],
        out_specs=vmem,
        scratch_shapes=[
            pltpu.VMEM((K_UNITS * HALF, HEAD_DIM), jnp.bfloat16),
            pltpu.VMEM((K_UNITS * HALF, 2 * HEAD_DIM), jnp.bfloat16),
            pltpu.VMEM((2, GROUP * HALF, HEAD_DIM), jnp.bfloat16),
            pltpu.VMEM((2, GROUP * HALF, HEAD_DIM), jnp.float32),
            pltpu.VMEM((2, GROUP * HALF, 2 * HEAD_DIM), jnp.float32),
        ],
        compiler_params=pltpu.CompilerParams(vmem_limit_bytes=40 * 1024 * 1024),
        cost_estimate=pl.CostEstimate(
            flops=2_400_000_000, bytes_accessed=4_000_000, transcendentals=5_000_000
        ),
        name="attend",
    )(scalars, columns, queries, keys_values)


def combine_kernel(parts_ref, out_ref):
    parts, rows = parts_ref.shape[:2]
    lane = lax.broadcasted_iota(jnp.int32, (rows, HEAD_DIM), 1)
    stats = [parts_ref[p, :, Q_COLS:].astype(jnp.float32) for p in range(parts)]
    for g in range(GROUP):
        chosen = (lane >= 3 * g) & (lane < 3 * g + 3)
        levels = [
            jnp.sum(jnp.where(chosen, s, 0.0), axis=1, keepdims=True) for s in stats
        ]
        highest = functools.reduce(jnp.maximum, levels)
        shares = [jnp.exp2(level - highest) for level in levels]
        inverse = 1.0 / sum(shares)
        columns = slice(g * HEAD_DIM, (g + 1) * HEAD_DIM)
        summed = sum(
            parts_ref[p, :, columns].astype(jnp.float32) * (shares[p] * inverse)
            for p in range(parts)
        )
        out_ref[:, columns] = summed.astype(jnp.bfloat16)


def combine(parts):
    vmem = pl.BlockSpec(memory_space=pltpu.VMEM)
    return pl.pallas_call(
        combine_kernel,
        out_shape=jax.ShapeDtypeStruct((parts.shape[1], Q_COLS), jnp.bfloat16),
        in_specs=[vmem],
        out_specs=vmem,
        name="combine",
    )(parts)


def exchange(blocks, axes):
    return lax.all_to_all(blocks, axes, split_axis=0, concat_axis=0, tiled=True)


def shards(queries, keys_values, span_order):
    rows = queries.shape[0]
    scalars, columns = plan(span_order)
    by_head = queries.reshape(rows, KV_HEADS, Q_COLS)
    packed = jnp.concatenate([by_head, keys_values], axis=2)
    packed = exchange(jnp.transpose(packed, (1, 0, 2)), HEAD_AXES)
    packed = packed.reshape(KV_HEADS * rows, Q_COLS + 2 * HEAD_DIM)
    my_queries = packed[:, :Q_COLS]
    my_keys = packed[:, Q_COLS:]
    all_keys = exchange(jnp.broadcast_to(my_keys[None], (16,) + my_keys.shape), KEY_AXES)
    all_queries = exchange(jnp.broadcast_to(my_queries[None], (4,) + my_queries.shape), "x")
    partial = attend(
        scalars,
        columns,
        all_queries.reshape(Q_UNITS * HALF, Q_COLS),
        all_keys.reshape(K_UNITS * HALF, 2 * HEAD_DIM),
    )
    partial = exchange(partial.reshape(4, KV_HEADS * rows, Q_COLS + HEAD_DIM), "x")
    output = combine(partial)
    output = exchange(output.reshape(KV_HEADS, rows, Q_COLS), HEAD_AXES)
    return jnp.transpose(output, (1, 0, 2)).reshape(rows, HEADS, HEAD_DIM)


def solution(mesh):
    fine = Mesh(mesh.devices.reshape(SIZES), AXES)
    placed = (P(AXES, None, None), P(AXES, None, None), P())
    return jax.shard_map(
        shards,
        mesh=fine,
        in_specs=placed,
        out_specs=P(AXES, None, None),
        check_vma=False,
    )
```

time: 455 us -> 157 us (0.35)
  the two profiles are of different devices: /device:TPU:1 before, /device:TPU:176 now
where the time goes in v1:
time: 157 us
  waiting for transfers between devices  56 us (36%)
  blocking collectives  44.6 us (28%)
  Pallas kernels  31.6 us (20%)
  starting transfers between devices  17.2 us (11%)
  local copies, waits for them, and re-layouts  5.01 us (3%)
  other arithmetic  2.03 us (1%)
    all_to_all x2, waiting for transfers between devices, exchange(): return lax.all_to_all(blocks, axes, split_axis=0, concat_axis=0, tiled=True)  56 us
    all_to_all x3, blocking collectives, exchange(): return lax.all_to_all(blocks, axes, split_axis=0, concat_axis=0, tiled=True)  44.6 us
    pallas_call x1, Pallas kernels, attend(): pl.pallas_call(attend_kernel, out_shape=jax.ShapeDtypeStruct((Q_UNITS * H...  29 us
    all_to_all x2, starting transfers between devices, exchange(): return lax.all_to_all(blocks, axes, split_axis=0, concat_axis=0, tiled=True)  17.2 us
  transfers between devices with their start and end apart: 2, of which 2 were waited for; matrix products, arithmetic and copies ran while one was open for 1% of the time, Pallas kernels for 0%

profile of v1, /device:TPU:176, one launch (start us, length us, event | category | flops | bytes accessed | tf_op | source)
XLA Modules:
  0.0 156.5 jit_solution(6132036948141371053)
XLA Ops:
  0.0 1.1 reshape.110
  1.1 0.9 maximum_bitcast_fusion
  2.0 0.1 copy.19
  2.0 10.8 %all_to_all.25 = bf16[8,24,768]{2,1,0:T(8,128)(2,1)S(1)} all-to-all(bf16[8,24,768]{2,1,0:T(8,128)(2,1)S(1)} %copy.19), channel_id=1, replica_groups=mesh['zh'=4,'zl'=2,'yl'=2,'x'=4,'yh'=4,'core'=2] {'zl','yl','core'}, dimensions={0} | all-to-all | bytes 589824 | tf_op jit(solution)/shard_map/all_to_all | solution.py:210
  12.9 0.9 broadcast_in_dim.102
  13.8 4.3 %all-to-all-start.1 = ((bf16[4,192,512]{2,1,0:T(8,128)(2,1)}), bf16[4,192,512]{2,1,0:T(8,128)(2,1)S(1)}, u32[]{:S(2)}, u32[]{:S(2)}) async-start(bf16[4,192,512]{2,1,0:T(8,128)(2,1)} %broadcast_in_dim.102), calls=%async_computation.1 | async-start | bytes 1572864 | tf_op jit(solution)/shard_map/all_to_all | solution.py:210
  18.1 12.4 %all-to-all-done.1 = bf16[4,192,512]{2,1,0:T(8,128)(2,1)S(1)} async-done(((bf16[4,192,512]{2,1,0:T(8,128)(2,1)}), bf16[4,192,512]{2,1,0:T(8,128)(2,1)S(1)}, u32[]{:S(2)}, u32[]{:S(2)}) %all-to-all-start.1) | async-done | bytes 786464 | tf_op jit(solution)/shard_map/all_to_all | solution.py:210
  30.5 1.3 broadcast_in_dim.103
  31.8 12.9 %all-to-all-start.2 = ((bf16[16,192,256]{2,1,0:T(8,128)(2,1)}), bf16[16,192,256]{2,1,0:T(8,128)(2,1)S(1)}, u32[]{:S(2)}, u32[]{:S(2)}) async-start(bf16[16,192,256]{2,1,0:T(8,128)(2,1)} %broadcast_in_dim.103), calls=%async_computation.2 | async-start | bytes 3145728 | tf_op jit(solution)/shard_map/all_to_all | solution.py:210
  44.7 0.0 copy-done
  44.7 0.2 reshape.109
  44.9 0.1 select_reduce_fusion.1
  45.0 0.1 select_reduce_fusion.6
  45.2 0.1 copy.18
  45.3 0.1 add.81
  45.4 0.1 copy.16
  45.5 0.1 add.76
  45.7 0.2 convert_reduce_fusion
  45.8 0.1 select_reduce_fusion
  46.0 0.1 iota_add_fusion
  46.0 0.1 add.85.columns
  46.1 0.2 convert_reduce_fusion.3
  46.3 0.1 select_reduce_fusion.4
  46.4 0.2 convert_reduce_fusion.1
  46.6 0.1 concatenate.6.scalars
  46.7 43.7 %all-to-all-done.2 = bf16[16,192,256]{2,1,0:T(8,128)(2,1)S(1)} async-done(((bf16[16,192,256]{2,1,0:T(8,128)(2,1)}), bf16[16,192,256]{2,1,0:T(8,128)(2,1)S(1)}, u32[]{:S(2)}, u32[]{:S(2)}) %all-to-all-start.2) | async-done | bytes 1572896 | tf_op jit(solution)/shard_map/all_to_all | solution.py:210
  90.3 29.0 %attend.1 = bf16[768,640]{1,0:T(8,128)(2,1)S(1)} custom-call(s32[128]{0:T(128)S(1)} %concatenate.6.scalars, s32[1,3072]{1,0:T(1,128)S(1)} %add.85.columns, bf16[768,512]{1,0:T(8,128)(2,1)S(1)} %bitcast.14, bf16[3072,256]{1,0:T(8,128)(2,1)S(1)} %bitcast.12), custom_call_target="tpu_custom_call" | custom-call | flops 2400000000 | bytes 4000000 | tf_op jit(solution)/shard_map/attend/pallas_call | solution.py:158
  119.4 18.5 %all_to_all.26.parts_ref = bf16[4,192,640]{2,1,0:T(8,128)(2,1)} all-to-all(bf16[4,192,640]{2,1,0:T(8,128)(2,1)S(1)} %bitcast.13), channel_id=1, replica_groups=mesh['zh'=4,'zl'=2,'yl'=2,'x'=4,'yh'=4,'core'=2] {'x'}, dimensions={0} | all-to-all | bytes 1966080 | tf_op jit(solution)/shard_map/all_to_all | solution.py:210
  137.9 2.6 %combine.1 = bf16[192,512]{1,0:T(8,128)(2,1)} custom-call(bf16[4,192,640]{2,1,0:T(8,128)(2,1)} %all_to_all.26.parts_ref), custom_call_target="tpu_custom_call" | custom-call | tf_op jit(solution)/shard_map/combine/pallas_call | solution.py:200
  140.4 15.2 %all_to_all.27 = bf16[8,24,512]{2,1,0:T(8,128)(2,1)S(1)} all-to-all(bf16[8,24,512]{2,1,0:T(8,128)(2,1)} %bitcast.17), channel_id=1, replica_groups=mesh['zh'=4,'zl'=2,'yl'=2,'x'=4,'yh'=4,'core'=2] {'zl','yl','core'}, dimensions={0} | all-to-all | bytes 393216 | tf_op jit(solution)/shard_map/all_to_all | solution.py:210
  155.7 0.1 copy.20
  155.7 0.8 reshape.116
  (9 shorter events, 0.1 us)
Async XLA Ops:
  13.8 16.7 %all-to-all-start.1 = ((bf16[4,192,512]{2,1,0:T(8,128)(2,1)}), bf16[4,192,512]{2,1,0:T(8,128)(2,1)S(1)}, u32[]{:S(2)}, u32[]{:S(2)}) async-start(bf16[4,192,512]{2,1,0:T(8,128)(2,1)} %broadcast_in_dim.102), calls=%async_computation.1 | async-start | bytes 1572864 | tf_op jit(solution)/shard_map/all_to_all | solution.py:210
  31.8 12.9 %copy-start = (s32[128]{0:T(128)S(1)}, s32[128]{0:T(128)}, u32[]{:S(2)}) copy-start(s32[128]{0:T(128)} %param.5) | copy-start | bytes 1540
  31.8 58.5 %all-to-all-start.2 = ((bf16[16,192,256]{2,1,0:T(8,128)(2,1)}), bf16[16,192,256]{2,1,0:T(8,128)(2,1)S(1)}, u32[]{:S(2)}, u32[]{:S(2)}) async-start(bf16[16,192,256]{2,1,0:T(8,128)(2,1)} %broadcast_in_dim.103), calls=%async_computation.2 | async-start | bytes 3145728 | tf_op jit(solution)/shard_map/all_to_all | solution.py:210

commit v2 on v1

v2 whole, which is shorter than its diff:
```python
import functools
import math

import jax
import jax.numpy as jnp
from jax import lax
from jax.experimental import pallas as pl
from jax.experimental.pallas import tpu as pltpu
from jax.sharding import Mesh, PartitionSpec as P

HEADS = 32
KV_HEADS = 8
GROUP = HEADS // KV_HEADS
HEAD_DIM = 128
SPAN = 96
QUARTER = 24
UNIT = 48
Q_HEADS = 2
SPANS = 32
KEYS = SPANS * SPAN
Q_ROWS = SPANS * UNIT
TOGETHER = 4
GROUP_ROWS = TOGETHER * Q_HEADS * UNIT
PARTS = 2
PART_ROWS = GROUP_ROWS // PARTS
WIDE = 512
NARROW = 256
Q_COLS = Q_HEADS * HEAD_DIM
BLOCK_ROWS = 384
STAT_ROWS = 32
EXPONENT = math.log2(math.e) / math.sqrt(HEAD_DIM)
LOWEST = -1e30

AXES = ("zh", "zl", "yl", "x", "yh", "core")
SIZES = (4, 2, 2, 4, 4, 2)
HEAD_AXES = ("zh", "yh")
QUERY_AXES = ("zl", "yl")

K_INDEX, Q_INDEX, Q_SORTED, BELOW, UPTO, CORE = 0, 32, 64, 96, 128, 160


def ranked(values):
    n = values.shape[0]
    rank = jnp.sum((values[None, :] < values[:, None]).astype(jnp.int32), axis=1)
    hit = rank[:, None] == jnp.arange(n)[None, :]
    index = jnp.sum(jnp.where(hit, jnp.arange(n)[:, None], 0), axis=0)
    return index, jnp.sum(jnp.where(hit, values[:, None], 0), axis=0)


def plan(span_order):
    order = span_order.reshape(4, 2, 2, 4, 2)
    x_is = lax.axis_index("x") == jnp.arange(4)
    zl_is = lax.axis_index("zl") == jnp.arange(2)
    yl_is = lax.axis_index("yl") == jnp.arange(2)
    near = zl_is[:, None, None, None] & yl_is[:, None, None]
    keys = jnp.sum(jnp.where(near, order, 0), axis=(1, 2))
    keys = jnp.transpose(keys, (1, 0, 2)).reshape(SPANS)
    queries = jnp.sum(jnp.where(x_is[:, None], order, 0), axis=3)
    queries = jnp.transpose(queries, (1, 2, 0, 3)).reshape(SPANS)
    k_index, k_sorted = ranked(keys)
    q_index, q_sorted = ranked(queries)
    below = jnp.sum((k_sorted[None, :] < q_sorted[:, None]).astype(jnp.int32), axis=1)
    upto = jnp.sum((k_sorted[None, :] <= q_sorted[:, None]).astype(jnp.int32), axis=1)
    core = jnp.full((SPANS,), lax.axis_index("core"), jnp.int32)
    scalars = jnp.concatenate([k_index, q_index, q_sorted, below, upto, core])
    row = jnp.arange(SPAN, dtype=jnp.int32)
    half, place = row // UNIT, row % UNIT
    offset = half * QUARTER + place + (place // QUARTER) * QUARTER
    columns = k_sorted[:, None] * SPAN + offset[None, :]
    return scalars.astype(jnp.int32), columns.reshape(1, KEYS).astype(jnp.int32)


def attend_kernel(
    scalars, columns, q_ref, kv_ref, out_ref,
    keys, values, q_group, q_position, scores, top, total, stats,
):
    values[:, HEAD_DIM:] = jnp.ones((KEYS, HEAD_DIM), jnp.bfloat16)

    def place(rank, _):
        for core in range(2):
            source = (core * SPANS + scalars[K_INDEX + rank]) * UNIT
            target = (2 * rank + core) * UNIT
            block = kv_ref[pl.ds(pl.multiple_of(source, UNIT), UNIT), :]
            target = pl.ds(pl.multiple_of(target, UNIT), UNIT)
            keys[target, :] = block[:, :HEAD_DIM]
            values[target, :HEAD_DIM] = block[:, HEAD_DIM:]
        return 0

    lax.fori_loop(0, SPANS, place, 0)

    row = lax.broadcasted_iota(jnp.int32, (UNIT, HEAD_DIM), 0)
    offset = row + jnp.where(row >= QUARTER, QUARTER, 0) + scalars[CORE] * QUARTER
    lane = lax.broadcasted_iota(jnp.int32, (UNIT, HEAD_DIM), 1)
    part_rows = [slice(p * PART_ROWS, (p + 1) * PART_ROWS) for p in range(PARTS)]

    def run_group(group, _):
        first = group * TOGETHER
        for u in range(TOGETHER):
            source = pl.multiple_of(scalars[Q_INDEX + first + u] * UNIT, UNIT)
            position = scalars[Q_SORTED + first + u] * SPAN + offset
            for g in range(Q_HEADS):
                to = slice((u * Q_HEADS + g) * UNIT, (u * Q_HEADS + g + 1) * UNIT)
                q_group[to, :] = q_ref[
                    pl.ds(source, UNIT), g * HEAD_DIM : (g + 1) * HEAD_DIM
                ]
                q_position[to, :] = position
        top[...] = jnp.full(top.shape, LOWEST, jnp.float32)
        total[...] = jnp.zeros(total.shape, jnp.float32)

        def score(start, width, masked):
            key_block = keys[pl.ds(start, width), :]
            for rows in part_rows:
                block = lax.dot_general(
                    q_group[rows, :],
                    key_block,
                    (((1,), (1,)), ((), ())),
                    preferred_element_type=jnp.float32,
                )
                tiles = []
                for t in range(width // HEAD_DIM):
                    tile = block[:, t * HEAD_DIM : (t + 1) * HEAD_DIM]
                    at = pl.multiple_of(start + t * HEAD_DIM, HEAD_DIM)
                    if masked:
                        allowed = columns[:, pl.ds(at, HEAD_DIM)] <= q_position[rows, :]
                        tile = jnp.where(allowed, tile, LOWEST)
                    scores[rows, pl.ds(at, HEAD_DIM)] = tile
                    tiles.append(tile)
                top[rows, :] = functools.reduce(jnp.maximum, tiles, top[rows, :])

        def weigh(start, width):
            value_block = values[pl.ds(start, width), :]
            for rows in part_rows:
                highest = top[rows, :]
                tiles = []
                for t in range(width // HEAD_DIM):
                    at = pl.multiple_of(start + t * HEAD_DIM, HEAD_DIM)
                    tile = (scores[rows, pl.ds(at, HEAD_DIM)] - highest) * EXPONENT
                    tiles.append(jnp.exp2(tile).astype(jnp.bfloat16))
                total[rows, :] += jnp.dot(
                    jnp.concatenate(tiles, axis=1),
                    value_block,
                    preferred_element_type=jnp.float32,
                )

        free = scalars[BELOW + first] * SPAN // WIDE
        ends = (scalars[UPTO + first + TOGETHER - 1] * SPAN + NARROW - 1) // NARROW

        def free_step(step, _):
            score(pl.multiple_of(step * WIDE, WIDE), WIDE, False)
            return 0

        def masked_step(step, _):
            score(pl.multiple_of(step * NARROW, NARROW), NARROW, True)
            return 0

        def wide_step(step, _):
            weigh(pl.multiple_of(step * WIDE, WIDE), WIDE)
            return 0

        def narrow_step(step, _):
            weigh(pl.multiple_of(step * NARROW, NARROW), NARROW)
            return 0

        ratio = WIDE // NARROW
        lax.fori_loop(0, free, free_step, 0)
        lax.fori_loop(free * ratio, ends, masked_step, 0)
        top[...] = jnp.broadcast_to(jnp.max(top[...], axis=1, keepdims=True), top.shape)
        lax.fori_loop(0, ends // ratio, wide_step, 0)
        lax.fori_loop(ends // ratio * ratio, ends, narrow_step, 0)

        for u in range(TOGETHER):
            unit = scalars[Q_INDEX + first + u]
            block, within = unit // 8, unit % 8
            target = block * (BLOCK_ROWS + STAT_ROWS) + within * UNIT
            target = pl.ds(pl.multiple_of(target, 16), UNIT)
            packed = jnp.zeros((UNIT, HEAD_DIM), jnp.float32)
            for g in range(Q_HEADS):
                part = slice((u * Q_HEADS + g) * UNIT, (u * Q_HEADS + g + 1) * UNIT)
                weight_sum = total[part, HEAD_DIM:]
                highest = top[part, :]
                some = (highest > LOWEST) & (weight_sum > 0.0)
                safe = jnp.where(some, weight_sum, 1.0)
                out_ref[target, g * HEAD_DIM : (g + 1) * HEAD_DIM] = (
                    total[part, :HEAD_DIM] / safe
                ).astype(jnp.bfloat16)
                level = jnp.where(some, highest * EXPONENT + jnp.log2(safe), LOWEST)
                high = level.astype(jnp.bfloat16).astype(jnp.float32)
                rest = level - high
                middle = rest.astype(jnp.bfloat16).astype(jnp.float32)
                low = rest - middle
                packed = jnp.where(lane == 3 * g, high, packed)
                packed = jnp.where(lane == 3 * g + 1, middle, packed)
                packed = jnp.where(lane == 3 * g + 2, low, packed)
            stats[pl.ds(pl.multiple_of(unit * UNIT, UNIT), UNIT), :] = packed.astype(
                jnp.bfloat16
            )
        return 0

    lax.fori_loop(0, SPANS // TOGETHER, run_group, 0)

    pick = (
        lax.broadcasted_iota(jnp.int32, (16, HEAD_DIM), 0)
        == lax.broadcasted_iota(jnp.int32, (16, HEAD_DIM), 1)
    ).astype(jnp.bfloat16)
    for block in range(Q_ROWS // BLOCK_ROWS):
        turned = lax.dot_general(
            pick,
            stats[block * BLOCK_ROWS : (block + 1) * BLOCK_ROWS, :],
            (((1,), (1,)), ((), ())),
            preferred_element_type=jnp.float32,
        ).astype(jnp.bfloat16)
        at = block * (BLOCK_ROWS + STAT_ROWS) + BLOCK_ROWS
        out_ref[at : at + 16, :] = turned[:, :Q_COLS]
        out_ref[at + 16 : at + 32, :HEAD_DIM] = turned[:, Q_COLS:]
        out_ref[at + 16 : at + 32, HEAD_DIM:] = jnp.zeros((16, HEAD_DIM), jnp.bfloat16)


def attend(scalars, columns, queries, keys_values):
    vmem = pl.BlockSpec(memory_space=pltpu.VMEM)
    blocks = Q_ROWS // BLOCK_ROWS
    return pl.pallas_call(
        attend_kernel,
        out_shape=jax.ShapeDtypeStruct((blocks * (BLOCK_ROWS + STAT_ROWS), Q_COLS), jnp.bfloat16),
        in_specs=[pl.BlockSpec(memory_space=pltpu.SMEM), vmem, vmem, vmem],
        out_specs=vmem,
        scratch_shapes=[
            pltpu.VMEM((KEYS, HEAD_DIM), jnp.bfloat16),
            pltpu.VMEM((KEYS, 2 * HEAD_DIM), jnp.bfloat16),
            pltpu.VMEM((GROUP_ROWS, HEAD_DIM), jnp.bfloat16),
            pltpu.VMEM((GROUP_ROWS, HEAD_DIM), jnp.int32),
            pltpu.VMEM((GROUP_ROWS, KEYS), jnp.float32),
            pltpu.VMEM((GROUP_ROWS, HEAD_DIM), jnp.float32),
            pltpu.VMEM((GROUP_ROWS, 2 * HEAD_DIM), jnp.float32),
            pltpu.VMEM((Q_ROWS, HEAD_DIM), jnp.bfloat16),
        ],
        compiler_params=pltpu.CompilerParams(vmem_limit_bytes=40 * 1024 * 1024),
        cost_estimate=pl.CostEstimate(
            flops=2_400_000_000, bytes_accessed=4_000_000, transcendentals=5_000_000
        ),
        name="attend",
    )(scalars, columns, queries, keys_values)


def combine_kernel(parts_ref, out_ref):
    parts = parts_ref.shape[0]
    row = lax.broadcasted_iota(jnp.int32, (16, Q_COLS), 0)
    head = lax.broadcasted_iota(jnp.int32, (16, Q_COLS), 1) // HEAD_DIM
    spread = ((row >= 3 * head) & (row < 3 * head + 3)).astype(jnp.bfloat16)
    levels = []
    for p in range(parts):
        at = BLOCK_ROWS
        turned = jnp.concatenate(
            [parts_ref[p, at : at + 16, :], parts_ref[p, at + 16 : at + 32, :HEAD_DIM]],
            axis=1,
        )
        levels.append(
            lax.dot_general(
                turned,
                spread,
                (((0,), (0,)), ((), ())),
                preferred_element_type=jnp.float32,
            )
        )
    highest = functools.reduce(jnp.maximum, levels)
    shares = [jnp.exp2(level - highest) for level in levels]
    summed = sum(
        parts_ref[p, :BLOCK_ROWS, :].astype(jnp.float32) * shares[p] for p in range(parts)
    )
    out_ref[...] = (summed / sum(shares)).astype(jnp.bfloat16)


def combine(parts):
    vmem = pl.BlockSpec(memory_space=pltpu.VMEM)
    return pl.pallas_call(
        combine_kernel,
        out_shape=jax.ShapeDtypeStruct((BLOCK_ROWS, Q_COLS), jnp.bfloat16),
        in_specs=[vmem],
        out_specs=vmem,
        name="combine",
    )(parts)


def exchange(blocks, axes):
    return lax.all_to_all(blocks, axes, split_axis=0, concat_axis=0, tiled=True)


def shards(queries, keys_values, span_order):
    rows = queries.shape[0]
    scalars, columns = plan(span_order)
    by_head = queries.reshape(rows, HEADS // Q_HEADS, Q_COLS)
    packed = jnp.concatenate([by_head, jnp.repeat(keys_values, 2, axis=1)], axis=2)
    packed = exchange(jnp.transpose(packed, (1, 0, 2)), HEAD_AXES)
    packed = packed.reshape(BLOCK_ROWS, Q_COLS + 2 * HEAD_DIM)
    my_queries = packed[:, :Q_COLS]
    my_keys = packed[:, Q_COLS:]
    some_keys = exchange(jnp.broadcast_to(my_keys[None], (4,) + my_keys.shape), "x")
    all_queries = exchange(
        jnp.broadcast_to(my_queries[None], (4,) + my_queries.shape), QUERY_AXES
    )
    all_keys = lax.all_gather(some_keys, "core", axis=0, tiled=True)
    partial = attend(
        scalars,
        columns,
        all_queries.reshape(Q_ROWS, Q_COLS),
        all_keys.reshape(KEYS, 2 * HEAD_DIM),
    )
    partial = partial.reshape(4, BLOCK_ROWS + STAT_ROWS, Q_COLS)
    output = combine(exchange(partial, QUERY_AXES))
    output = exchange(output.reshape(HEADS // Q_HEADS, rows, Q_COLS), HEAD_AXES)
    return jnp.transpose(output, (1, 0, 2)).reshape(rows, HEADS, HEAD_DIM)


def solution(mesh):
    fine = Mesh(mesh.devices.reshape(SIZES), AXES)
    placed = (P(AXES, None, None), P(AXES, None, None), P())
    return jax.shard_map(
        shards,
        mesh=fine,
        in_specs=placed,
        out_specs=P(AXES, None, None),
        check_vma=False,
    )
```

time: 157 us -> 147 us (0.936)
  the two profiles are of different devices: /device:TPU:176 before, /device:TPU:1 now
where the time goes in v2:
time: 147 us; the launch traced here: 145 us
  blocking collectives  69.3 us (47%)
  Pallas kernels  25.2 us (17%)
  waiting for transfers between devices  20.4 us (14%)
  between operations  13.5 us (9%)
  local copies, waits for them, and re-layouts  7.8 us (5%)
  starting transfers between devices  7.51 us (5%)
    all_to_all x3, blocking collectives, exchange(): return lax.all_to_all(blocks, axes, split_axis=0, concat_axis=0, tiled=True)  69.3 us
    pallas_call x1, Pallas kernels, attend(): pl.pallas_call(attend_kernel, out_shape=jax.ShapeDtypeStruct((blocks * (B...  22.7 us
    all_to_all x2, waiting for transfers between devices, exchange(): return lax.all_to_all(blocks, axes, split_axis=0, concat_axis=0, tiled=True)  15.6 us
    all_to_all x2, starting transfers between devices, exchange(): return lax.all_to_all(blocks, axes, split_axis=0, concat_axis=0, tiled=True)  7.51 us
    all_gather x1, waiting for transfers between devices, shards(): all_keys = lax.all_gather(some_keys, 'core', axis=0, tiled=True)  4.83 us
  transfers between devices with their start and end apart: 3, of which 3 were waited for; matrix products, arithmetic and copies ran while one was open for 2% of the time, Pallas kernels for 0%

profile of v2, /device:TPU:1, one launch (start us, length us, event | category | flops | bytes accessed | tf_op | source)
XLA Modules:
  0.0 144.8 jit_solution(8969013608475627099)
XLA Ops:
  6.5 1.0 reshape.125
  7.5 1.0 broadcast_in_dim.87
  8.5 0.1 reshape.126
  8.7 0.2 copy.15
  8.9 31.7 %all_to_all.25 = bf16[16,24,512]{2,1,0:T(8,128)(2,1)S(1)} all-to-all(bf16[16,24,512]{2,1,0:T(8,128)(2,1)S(1)} %copy.15), channel_id=1, replica_groups=mesh['zh'=4,'zl'=2,'yl'=2,'x'=4,'yh'=4,'core'=2] {'zh','yh'}, dimensions={0} | all-to-all | bytes 786432 | tf_op jit(solution)/shard_map/all_to_all | solution.py:284
  40.7 0.9 broadcast_in_dim.89
  41.6 4.0 %all-to-all-start.2 = ((bf16[4,384,256]{2,1,0:T(8,128)(2,1)}), bf16[4,384,256]{2,1,0:T(8,128)(2,1)S(1)}, u32[]{:S(2)}, u32[]{:S(2)}) async-start(bf16[4,384,256]{2,1,0:T(8,128)(2,1)} %broadcast_in_dim.89), calls=%async_computation.2 | async-start | bytes 1572864 | tf_op jit(solution)/shard_map/all_to_all | solution.py:284
  45.6 0.2 reshape.124
  45.8 9.6 %all-to-all-done.2 = bf16[4,384,256]{2,1,0:T(8,128)(2,1)S(1)} async-done(((bf16[4,384,256]{2,1,0:T(8,128)(2,1)}), bf16[4,384,256]{2,1,0:T(8,128)(2,1)S(1)}, u32[]{:S(2)}, u32[]{:S(2)}) %all-to-all-start.2) | async-done | bytes 786464 | tf_op jit(solution)/shard_map/all_to_all | solution.py:284
  55.3 0.9 copy-done.1
  56.3 0.1 broadcast_and_fusion
  56.3 0.9 broadcast_in_dim.88
  57.3 3.5 %all-to-all-start.1 = ((bf16[4,384,256]{2,1,0:T(8,128)(2,1)}), bf16[4,384,256]{2,1,0:T(8,128)(2,1)S(1)}, u32[]{:S(2)}, u32[]{:S(2)}) async-start(bf16[4,384,256]{2,1,0:T(8,128)(2,1)} %broadcast_in_dim.88), calls=%async_computation.1 | async-start | bytes 1572864 | tf_op jit(solution)/shard_map/all_to_all | solution.py:284
  60.8 0.1 select_reduce_fusion
  60.9 0.1 lt.53
  61.0 0.1 lt.49
  61.1 0.2 convert_reduce_fusion.3
  61.3 0.1 select_reduce_fusion.2
  61.4 0.1 broadcast_add_fusion
  61.5 0.1 add.63.columns
  61.6 0.2 convert_reduce_fusion.2
  61.8 0.1 select_reduce_fusion.3
  61.9 0.2 convert_reduce_fusion
  62.1 0.1 concatenate.6.scalars
  62.2 6.0 %all-to-all-done.1 = bf16[4,384,256]{2,1,0:T(8,128)(2,1)S(1)} async-done(((bf16[4,384,256]{2,1,0:T(8,128)(2,1)}), bf16[4,384,256]{2,1,0:T(8,128)(2,1)S(1)}, u32[]{:S(2)}, u32[]{:S(2)}) %all-to-all-start.1) | async-done | bytes 786464 | tf_op jit(solution)/shard_map/all_to_all | solution.py:284
  68.2 4.8 %all-gather.2.cloned.1.call-done = bf16[8,384,256]{2,1,0:T(8,128)(2,1)} async-done(((bf16[4,384,256]{2,1,0:T(8,128)(2,1)}), bf16[8,384,256]{2,1,0:T(8,128)(2,1)}) %all-gather.2.cloned.1.call-update) | async-done | bytes 1572880 | tf_op jit(solution)/shard_map/all_gather | solution.py:300
  73.0 1.4 copy-done
  74.4 22.7 %attend.1 = bf16[1664,256]{1,0:T(8,128)(2,1)S(1)} custom-call(s32[192]{0:T(256)S(1)} %concatenate.6.scalars, s32[1,3072]{1,0:T(1,128)S(1)} %add.63.columns, bf16[1536,256]{1,0:T(8,128)(2,1)S(1)} %bitcast.11, bf16[3072,256]{1,0:T(8,128)(2,1)S(1)} %bitcast.12), custom_call_target="tpu_custom_call" | custom-call | flops 2400000000 | bytes 4000000 | tf_op jit(solution)/shard_map/attend/pallas_call | solution.py:221
  97.1 15.7 %all_to_all.26.parts_ref = bf16[4,416,256]{2,1,0:T(8,128)(2,1)} all-to-all(bf16[4,416,256]{2,1,0:T(8,128)(2,1)S(1)} %bitcast.10), channel_id=1, replica_groups=mesh['zh'=4,'zl'=2,'yl'=2,'x'=4,'yh'=4,'core'=2] {'zl','yl'}, dimensions={0} | all-to-all | bytes 1703936 | tf_op jit(solution)/shard_map/all_to_all | solution.py:284
  112.8 2.5 %combine.1 = bf16[384,256]{1,0:T(8,128)(2,1)} custom-call(bf16[4,416,256]{2,1,0:T(8,128)(2,1)} %all_to_all.26.parts_ref), custom_call_target="tpu_custom_call" | custom-call | tf_op jit(solution)/shard_map/combine/pallas_call | solution.py:274
  115.3 21.8 %all_to_all.27 = bf16[16,24,256]{2,1,0:T(8,128)(2,1)S(1)} all-to-all(bf16[16,24,256]{2,1,0:T(8,128)(2,1)} %bitcast.14), channel_id=1, replica_groups=mesh['zh'=4,'zl'=2,'yl'=2,'x'=4,'yh'=4,'core'=2] {'zh','yh'}, dimensions={0} | all-to-all | bytes 393216 | tf_op jit(solution)/shard_map/all_to_all | solution.py:284
  137.2 0.7 reshape.132
  (16 shorter events, 0.2 us)
Async XLA Ops:
  40.6 5.0 %copy-start.2 = (s32[128]{0:T(128)S(1)}, s32[128]{0:T(128)}, u32[]{:S(2)}) copy-start(s32[128]{0:T(128)} %param.5) | copy-start | bytes 1540
  41.6 13.8 %all-to-all-start.2 = ((bf16[4,384,256]{2,1,0:T(8,128)(2,1)}), bf16[4,384,256]{2,1,0:T(8,128)(2,1)S(1)}, u32[]{:S(2)}, u32[]{:S(2)}) async-start(bf16[4,384,256]{2,1,0:T(8,128)(2,1)} %broadcast_in_dim.89), calls=%async_computation.2 | async-start | bytes 1572864 | tf_op jit(solution)/shard_map/all_to_all | solution.py:284
  45.6 27.4 %all-gather.2.cloned.1.call-start = ((), (), s32[]{:S(2)}) async-start(), calls=%async_computation.5 | async-start | bytes 2359296 | tf_op jit(solution)/shard_map/all_gather | solution.py:300
  55.3 0.9 copy-start.1
  57.3 10.9 %all-to-all-start.1 = ((bf16[4,384,256]{2,1,0:T(8,128)(2,1)}), bf16[4,384,256]{2,1,0:T(8,128)(2,1)S(1)}, u32[]{:S(2)}, u32[]{:S(2)}) async-start(bf16[4,384,256]{2,1,0:T(8,128)(2,1)} %broadcast_in_dim.88), calls=%async_computation.1 | async-start | bytes 1572864 | tf_op jit(solution)/shard_map/all_to_all | solution.py:284
  73.0 1.4 copy-start
Sparse Core Ops, SparseCore 0:
  56.4 16.5 all-gather.1

commit v3 on v2

v3 whole, which is shorter than its diff:
```python
import functools
import math

import jax
import jax.numpy as jnp
from jax import lax
from jax.experimental import pallas as pl
from jax.experimental.pallas import tpu as pltpu
from jax.sharding import Mesh, PartitionSpec as P

HEADS = 32
KV_HEADS = 8
GROUP = HEADS // KV_HEADS
HEAD_DIM = 128
SPAN = 96
QUARTER = 24
UNIT = 48
K_SPANS = 32
KEYS = K_SPANS * SPAN
Q_UNITS = 16
Q_ROWS = Q_UNITS * UNIT
TOGETHER = 4
GROUP_ROWS = TOGETHER * GROUP * UNIT
PARTS = 2
PART_ROWS = GROUP_ROWS // PARTS
CHUNK = 1024
CHUNKS = KEYS // CHUNK
Q_COLS = GROUP * HEAD_DIM
BLOCK_ROWS = 192
STAT_ROWS = 16
EXPONENT = math.log2(math.e) / math.sqrt(HEAD_DIM)
LOWEST = -1e30

AXES = ("z2", "z1", "zl", "yl", "x", "y2", "y1", "core")
SIZES = (2, 2, 2, 2, 4, 2, 2, 2)
HEAD_AXES = ("zl", "yl", "y1")
QUERY_AXES = ("x",)
KEY_AXES = ("z2", "z1", "zl", "yl", "y2", "y1")

K_INDEX, Q_INDEX, Q_SORTED, BELOW, UPTO, HERE = 0, 32, 48, 64, 80, 96


def ranked(values):
    n = values.shape[0]
    rank = jnp.sum((values[None, :] < values[:, None]).astype(jnp.int32), axis=1)
    hit = rank[:, None] == jnp.arange(n)[None, :]
    index = jnp.sum(jnp.where(hit, jnp.arange(n)[:, None], 0), axis=0)
    return index, jnp.sum(jnp.where(hit, values[:, None], 0), axis=0)


def plan(span_order, place):
    order = span_order.reshape(4, 4, 4, 2)
    x_is = place["x"] == jnp.arange(4)
    far = place["z2"] * 2 + place["z1"] == jnp.arange(4)
    half = place["y2"] == jnp.arange(2)
    keys = jnp.sum(jnp.where(x_is[:, None], order, 0), axis=2).reshape(K_SPANS)
    mine = far[:, None, None, None] & half
    queries = jnp.sum(jnp.where(mine, order, 0), axis=(0, 3))
    source = (place["x"] - jnp.arange(4)) % 4
    picked = source[:, None] == jnp.arange(4)
    queries = jnp.sum(jnp.where(picked[:, None, :], queries[None], 0), axis=2)
    queries = queries.reshape(Q_UNITS)
    k_index, k_sorted = ranked(keys)
    q_index, q_sorted = ranked(queries)
    below = jnp.sum((k_sorted[None, :] < q_sorted[:, None]).astype(jnp.int32), axis=1)
    upto = jnp.sum((k_sorted[None, :] <= q_sorted[:, None]).astype(jnp.int32), axis=1)
    here = jnp.full((Q_UNITS,), place["core"] * 4 + place["x"], jnp.int32)
    scalars = jnp.concatenate([k_index, q_index, q_sorted, below, upto, here])
    row = jnp.arange(SPAN, dtype=jnp.int32)
    core = jnp.where(row < UNIT, place["core"], 1 - place["core"])
    within = row % UNIT
    offset = core * QUARTER + within + (within // QUARTER) * QUARTER
    columns = k_sorted[:, None] * SPAN + offset[None, :]
    return scalars.astype(jnp.int32), columns.reshape(CHUNKS, 1, CHUNK).astype(jnp.int32)


def attend_kernel(
    scalars, columns, q0_ref, q1_ref, q2_ref, q3_ref, own_ref, other_ref, out_ref,
    q_ref, sorted_kv, keys_t, values, q_group, q_position, scores, top, total, stats,
):
    for block, block_ref in enumerate((q0_ref, q1_ref, q2_ref, q3_ref)):
        q_ref[block * BLOCK_ROWS : (block + 1) * BLOCK_ROWS, :] = block_ref[...]

    def place(rank, _):
        source = pl.multiple_of(scalars[K_INDEX + rank] * UNIT, UNIT)
        for half, kv_ref in enumerate((own_ref, other_ref)):
            target = pl.ds(pl.multiple_of((2 * rank + half) * UNIT, UNIT), UNIT)
            sorted_kv[target, :] = kv_ref[pl.ds(source, UNIT), :]
        return 0

    lax.fori_loop(0, K_SPANS, place, 0)
    for chunk in range(CHUNKS):
        rows = slice(chunk * CHUNK, (chunk + 1) * CHUNK)
        keys_t[chunk] = sorted_kv[rows, :HEAD_DIM].T
        values[chunk, :, :HEAD_DIM] = sorted_kv[rows, HEAD_DIM:]
        values[chunk, :, HEAD_DIM:] = jnp.ones((CHUNK, HEAD_DIM), jnp.bfloat16)

    row = lax.broadcasted_iota(jnp.int32, (UNIT, HEAD_DIM), 0)
    offset = row + jnp.where(row >= QUARTER, QUARTER, 0) + scalars[HERE] // 4 * QUARTER
    lane = lax.broadcasted_iota(jnp.int32, (UNIT, HEAD_DIM), 1)
    part_rows = [slice(p * PART_ROWS, (p + 1) * PART_ROWS) for p in range(PARTS)]

    def run_group(group, _):
        first = group * TOGETHER
        for u in range(TOGETHER):
            source = pl.multiple_of(scalars[Q_INDEX + first + u] * UNIT, UNIT)
            position = scalars[Q_SORTED + first + u] * SPAN + offset
            for g in range(GROUP):
                to = slice((u * GROUP + g) * UNIT, (u * GROUP + g + 1) * UNIT)
                q_group[to, :] = q_ref[
                    pl.ds(source, UNIT), g * HEAD_DIM : (g + 1) * HEAD_DIM
                ]
                q_position[to, :] = position
        top[...] = jnp.full(top.shape, LOWEST, jnp.float32)
        total[...] = jnp.zeros(total.shape, jnp.float32)

        def score(chunk, masked):
            for rows in part_rows:
                block = jnp.dot(
                    q_group[rows, :], keys_t[chunk], preferred_element_type=jnp.float32
                )
                if masked:
                    position = q_position[rows, :]
                    tiles = [
                        jnp.where(
                            columns[chunk, :, t : t + HEAD_DIM] <= position,
                            block[:, t : t + HEAD_DIM],
                            LOWEST,
                        )
                        for t in range(0, CHUNK, HEAD_DIM)
                    ]
                    block = jnp.concatenate(tiles, axis=1)
                else:
                    tiles = [block[:, t : t + HEAD_DIM] for t in range(0, CHUNK, HEAD_DIM)]
                scores[chunk, rows, :] = block
                top[rows, :] = functools.reduce(jnp.maximum, tiles, top[rows, :])

        def weigh(chunk):
            for rows in part_rows:
                highest = top[rows, :]
                tiles = [
                    jnp.exp2((scores[chunk, rows, t : t + HEAD_DIM] - highest) * EXPONENT)
                    for t in range(0, CHUNK, HEAD_DIM)
                ]
                total[rows, :] += jnp.dot(
                    jnp.concatenate(tiles, axis=1).astype(jnp.bfloat16),
                    values[chunk],
                    preferred_element_type=jnp.float32,
                )

        free = scalars[BELOW + first] * SPAN // CHUNK
        ends = (scalars[UPTO + first + TOGETHER - 1] * SPAN + CHUNK - 1) // CHUNK

        def free_step(chunk, _):
            score(chunk, False)
            return 0

        def masked_step(chunk, _):
            score(chunk, True)
            return 0

        def weigh_step(chunk, _):
            weigh(chunk)
            return 0

        lax.fori_loop(0, free, free_step, 0)
        lax.fori_loop(free, ends, masked_step, 0)
        top[...] = jnp.broadcast_to(jnp.max(top[...], axis=1, keepdims=True), top.shape)
        lax.fori_loop(0, ends, weigh_step, 0)

        for u in range(TOGETHER):
            unit = scalars[Q_INDEX + first + u]
            block, within = (scalars[HERE] - unit // 4) % 4, unit % 4
            target = block * (BLOCK_ROWS + STAT_ROWS) + within * UNIT
            target = pl.ds(pl.multiple_of(target, 16), UNIT)
            packed = jnp.zeros((UNIT, HEAD_DIM), jnp.float32)
            for g in range(GROUP):
                part = slice((u * GROUP + g) * UNIT, (u * GROUP + g + 1) * UNIT)
                weight_sum = total[part, HEAD_DIM:]
                highest = top[part, :]
                some = (highest > LOWEST) & (weight_sum > 0.0)
                safe = jnp.where(some, weight_sum, 1.0)
                out_ref[target, g * HEAD_DIM : (g + 1) * HEAD_DIM] = (
                    total[part, :HEAD_DIM] / safe
                ).astype(jnp.bfloat16)
                level = jnp.where(some, highest * EXPONENT + jnp.log2(safe), LOWEST)
                high = level.astype(jnp.bfloat16).astype(jnp.float32)
                rest = level - high
                middle = rest.astype(jnp.bfloat16).astype(jnp.float32)
                low = rest - middle
                packed = jnp.where(lane == 3 * g, high, packed)
                packed = jnp.where(lane == 3 * g + 1, middle, packed)
                packed = jnp.where(lane == 3 * g + 2, low, packed)
            target = pl.ds(pl.multiple_of(block * BLOCK_ROWS + within * UNIT, UNIT), UNIT)
            stats[target, :] = packed.astype(jnp.bfloat16)
        return 0

    lax.fori_loop(0, Q_UNITS // TOGETHER, run_group, 0)

    pick = (
        lax.broadcasted_iota(jnp.int32, (16, HEAD_DIM), 0)
        == lax.broadcasted_iota(jnp.int32, (16, HEAD_DIM), 1)
    ).astype(jnp.bfloat16)
    for block in range(Q_ROWS // BLOCK_ROWS):
        turned = lax.dot_general(
            pick,
            stats[block * BLOCK_ROWS : (block + 1) * BLOCK_ROWS, :],
            (((1,), (1,)), ((), ())),
            preferred_element_type=jnp.float32,
        ).astype(jnp.bfloat16)
        at = block * (BLOCK_ROWS + STAT_ROWS) + BLOCK_ROWS
        out_ref[at : at + STAT_ROWS, :BLOCK_ROWS] = turned
        out_ref[at : at + STAT_ROWS, BLOCK_ROWS:] = jnp.zeros(
            (STAT_ROWS, Q_COLS - BLOCK_ROWS), jnp.bfloat16
        )


def attend(scalars, columns, *arrays):
    vmem = pl.BlockSpec(memory_space=pltpu.VMEM)
    blocks = Q_ROWS // BLOCK_ROWS
    return pl.pallas_call(
        attend_kernel,
        out_shape=jax.ShapeDtypeStruct((blocks * (BLOCK_ROWS + STAT_ROWS), Q_COLS), jnp.bfloat16),
        in_specs=[pl.BlockSpec(memory_space=pltpu.SMEM)] + [vmem] * 7,
        out_specs=vmem,
        scratch_shapes=[
            pltpu.VMEM((Q_ROWS, Q_COLS), jnp.bfloat16),
            pltpu.VMEM((KEYS, 2 * HEAD_DIM), jnp.bfloat16),
            pltpu.VMEM((CHUNKS, HEAD_DIM, CHUNK), jnp.bfloat16),
            pltpu.VMEM((CHUNKS, CHUNK, 2 * HEAD_DIM), jnp.bfloat16),
            pltpu.VMEM((GROUP_ROWS, HEAD_DIM), jnp.bfloat16),
            pltpu.VMEM((GROUP_ROWS, HEAD_DIM), jnp.int32),
            pltpu.VMEM((CHUNKS, GROUP_ROWS, CHUNK), jnp.float32),
            pltpu.VMEM((GROUP_ROWS, HEAD_DIM), jnp.float32),
            pltpu.VMEM((GROUP_ROWS, 2 * HEAD_DIM), jnp.float32),
            pltpu.VMEM((Q_ROWS, HEAD_DIM), jnp.bfloat16),
        ],
        compiler_params=pltpu.CompilerParams(vmem_limit_bytes=40 * 1024 * 1024),
        cost_estimate=pl.CostEstimate(
            flops=2_400_000_000, bytes_accessed=4_000_000, transcendentals=5_000_000
        ),
        name="attend",
    )(scalars, columns, *arrays)


def combine_kernel(parts_ref, out_ref):
    parts = parts_ref.shape[0]
    row = lax.broadcasted_iota(jnp.int32, (16, Q_COLS), 0)
    head = lax.broadcasted_iota(jnp.int32, (16, Q_COLS), 1) // HEAD_DIM
    spread = ((row >= 3 * head) & (row < 3 * head + 3)).astype(jnp.bfloat16)
    levels = []
    for p in range(parts):
        turned = parts_ref[p, BLOCK_ROWS:, :BLOCK_ROWS]
        levels.append(
            lax.dot_general(
                turned,
                spread,
                (((0,), (0,)), ((), ())),
                preferred_element_type=jnp.float32,
            )
        )
    highest = functools.reduce(jnp.maximum, levels)
    shares = [jnp.exp2(level - highest) for level in levels]
    summed = sum(
        parts_ref[p, :BLOCK_ROWS, :].astype(jnp.float32) * shares[p] for p in range(parts)
    )
    out_ref[...] = (summed / sum(shares)).astype(jnp.bfloat16)


def combine(parts):
    vmem = pl.BlockSpec(memory_space=pltpu.VMEM)
    return pl.pallas_call(
        combine_kernel,
        out_shape=jax.ShapeDtypeStruct((BLOCK_ROWS, Q_COLS), jnp.bfloat16),
        in_specs=[vmem],
        out_specs=vmem,
        name="combine",
    )(parts)


def exchange(blocks, axes):
    return lax.all_to_all(blocks, axes, split_axis=0, concat_axis=0, tiled=True)


def spread(blocks, axes, chosen):
    sizes = [SIZES[AXES.index(a)] for a in axes]
    lead = [n if a in chosen else 1 for a, n in zip(axes, sizes)]
    shape = blocks.shape[1:]
    blocks = jnp.broadcast_to(blocks.reshape(*lead, *shape), (*sizes, *shape))
    return blocks.reshape(math.prod(sizes), *shape)


def turn(block, axis, step):
    size = SIZES[AXES.index(axis)]
    return lax.ppermute(block, axis, [(i, (i + step) % size) for i in range(size)])


def shards(queries, keys_values, span_order):
    rows = queries.shape[0]
    scalars, columns = plan(span_order, {a: lax.axis_index(a) for a in AXES})
    by_head = jnp.transpose(queries.reshape(rows, KV_HEADS, Q_COLS), (1, 0, 2))
    mine = exchange(by_head, HEAD_AXES).reshape(BLOCK_ROWS, Q_COLS)
    own = jnp.transpose(keys_values, (1, 0, 2))
    mine, own = lax.optimization_barrier((mine, own))
    own = spread(own, KEY_AXES, HEAD_AXES)
    own = exchange(own, KEY_AXES).reshape(KEYS // 2, 2 * HEAD_DIM)
    gathered = [mine] + [turn(mine, "x", step) for step in range(1, 4)]
    own, *gathered = lax.optimization_barrier((own, *gathered))
    other = turn(own, "core", 1)
    partial = attend(scalars, columns, *gathered, own, other)
    partial = partial.reshape(4, BLOCK_ROWS + STAT_ROWS, Q_COLS)
    output = combine(exchange(partial, QUERY_AXES))
    output = exchange(output.reshape(KV_HEADS, rows, Q_COLS), HEAD_AXES)
    return jnp.transpose(output, (1, 0, 2)).reshape(rows, HEADS, HEAD_DIM)


def solution(mesh):
    fine = Mesh(mesh.devices.reshape(SIZES), AXES)
    placed = (P(AXES, None, None), P(AXES, None, None), P())
    return jax.shard_map(
        shards,
        mesh=fine,
        in_specs=placed,
        out_specs=P(AXES, None, None),
        check_vma=False,
    )
```

time: 147 us -> 107 us (0.73); the launches traced: 145 us -> 106 us
  blocking collectives: 69.3 us -> 41.9 us
  starting transfers between devices: 7.51 us -> 28.5 us
  between operations: 13.5 us -> 0.17 us
  waiting for transfers between devices: 20.4 us -> 12.4 us
  Pallas kernels: 25.2 us -> 17.9 us
  local copies, waits for them, and re-layouts: 7.8 us -> 4.1 us
    all_to_all x3, blocking collectives: 69.3 us -> 41.9 us  [exchange(): return lax.all_to_all(blocks, axes, split_axis=0, concat_axis=0, tiled=True)]
    ppermute x0 -> x4, starting transfers between devices: none -> 15.8 us  [turn(): lax.ppermute(block, axis, [(i, (i + step) % size) for i in range(size)])]
    all_to_all x2 -> x1, waiting for transfers between devices: 15.6 us -> 5.12 us  [exchange(): return lax.all_to_all(blocks, axes, split_axis=0, concat_axis=0, tiled=True)]
    pallas_call x1, Pallas kernels: 22.7 us -> 15.3 us  [attend(): pl.pallas_call(attend_kernel, out_shape=jax.ShapeDtypeStruct((blocks * (B...]
    ppermute x0 -> x4, waiting for transfers between devices: none -> 7.32 us  [turn(): lax.ppermute(block, axis, [(i, (i + step) % size) for i in range(size)])]
    all_to_all x2 -> x1, starting transfers between devices: 7.51 us -> 12.7 us  [exchange(): return lax.all_to_all(blocks, axes, split_axis=0, concat_axis=0, tiled=True)]
    all_gather x1 -> x0, waiting for transfers between devices: 4.83 us -> none  [shards(): all_keys = lax.all_gather(some_keys, 'core', axis=0, tiled=True)]
    broadcast_in_dim x4 -> x3, local copies, waits for them, and re-layouts: 2.88 us -> 0.96 us  [the longest x2 0.96 us: spread(): blocks = jnp.broadcast_to(blocks.reshape(*lead, *shape), (*sizes, *shape))]
  transfers between devices with their start and end apart: 3 -> 5, of which waited for: 3 -> 4; matrix products, arithmetic and copies ran while one was open for 2% -> 2% of each run, Pallas kernels for 0% -> 0%
where the time goes in v3:
time: 107 us; the launch traced here: 106 us
  blocking collectives  41.9 us (39%)
  starting transfers between devices  28.5 us (27%)
  Pallas kernels  17.9 us (17%)
  waiting for transfers between devices  12.4 us (12%)
  local copies, waits for them, and re-layouts  4.1 us (4%)
  other arithmetic  1.33 us (1%)
    all_to_all x3, blocking collectives, exchange(): return lax.all_to_all(blocks, axes, split_axis=0, concat_axis=0, tiled=True)  41.9 us
    ppermute x4, starting transfers between devices, turn(): lax.ppermute(block, axis, [(i, (i + step) % size) for i in range(size)])  15.8 us
    pallas_call x1, Pallas kernels, attend(): pl.pallas_call(attend_kernel, out_shape=jax.ShapeDtypeStruct((blocks * (B...  15.3 us
    all_to_all x1, starting transfers between devices, exchange(): return lax.all_to_all(blocks, axes, split_axis=0, concat_axis=0, tiled=True)  12.7 us
    ppermute x4, waiting for transfers between devices, turn(): lax.ppermute(block, axis, [(i, (i + step) % size) for i in range(size)])  7.32 us
    all_to_all x1, waiting for transfers between devices, exchange(): return lax.all_to_all(blocks, axes, split_axis=0, concat_axis=0, tiled=True)  5.12 us
    pallas_call x1, Pallas kernels, combine(): pl.pallas_call(combine_kernel, out_shape=jax.ShapeDtypeStruct((BLOCK_ROWS...  2.52 us
  transfers between devices with their start and end apart: 5, of which 4 were waited for; matrix products, arithmetic and copies ran while one was open for 2% of the time, Pallas kernels for 0%

profile of v3, /device:TPU:1, one launch (start us, length us, event | category | flops | bytes accessed | tf_op | source)
XLA Modules:
  0.0 106.3 jit_solution(1640122317007528137)
XLA Ops:
  0.0 1.1 reshape.153
  1.1 14.2 %all_to_all.20 = bf16[8,24,512]{2,1,0:T(8,128)(2,1)S(1)} all-to-all(bf16[8,24,512]{2,1,0:T(8,128)(2,1)S(1)} %bitcast.19), channel_id=1, replica_groups=mesh['z2'=2,'z1'=2,'zl'=2,'yl'=2,'x'=4,'y2'=2,'y1'=2,'core'=2] {'zl','yl..., dimensions={0} | all-to-all | bytes 393216 | tf_op jit(solution)/shard_map/all_to_all | solution.py:282
  15.3 0.9 broadcast_in_dim.125
  16.3 12.7 %all-to-all-start.1 = ((bf16[64,24,256]{2,1,0:T(8,128)(2,1)}), bf16[64,24,256]{2,1,0:T(8,128)(2,1)S(1)}, u32[]{:S(2)}, u32[]{:S(2)}) async-start(bf16[64,24,256]{2,1,0:T(8,128)(2,1)} %bitcast.4), calls=%async_computation.1 | async-start | bytes 1572864 | tf_op jit(solution)/shard_map/all_to_all | solution.py:282
  29.0 0.6 copy-done.1
  29.7 0.2 reshape.152
  29.9 0.1 broadcast_and_fusion
  30.0 0.2 select_reduce_fusion
  30.1 0.1 iota_compare_fusion.2
  30.2 0.2 select_reduce_fusion.6
  30.4 0.1 lt.72
  30.4 0.1 lt.67
  30.5 0.2 convert_reduce_fusion
  30.7 4.4 %collective-permute-start.2 = (bf16[192,512]{1,0:T(8,128)(2,1)S(1)}, bf16[192,512]{1,0:T(8,128)(2,1)S(1)}, u32[]{:S(2)}, u32[]{:S(2)}) collective-permute-start(bf16[192,512]{1,0:T(8,128)(2,1)S(1)} %bitcast.14), channel_id=1, source_target_pairs={{0,24},{8,0},{16,8},{24,16},{1,25},{9,1},{17,9},{25,17},{2,26},{10... | collective-permute-start | bytes 589832 | tf_op jit(solution)/shard_map/ppermute | solution.py:295
  35.1 2.4 %collective-permute-start.1 = (bf16[192,512]{1,0:T(8,128)(2,1)S(1)}, bf16[192,512]{1,0:T(8,128)(2,1)S(1)}, u32[]{:S(2)}, u32[]{:S(2)}) collective-permute-start(bf16[192,512]{1,0:T(8,128)(2,1)S(1)} %bitcast.15), channel_id=1, source_target_pairs={{0,16},{8,24},{16,0},{24,8},{1,17},{9,25},{17,1},{25,9},{2,18},{10... | collective-permute-start | bytes 589832 | tf_op jit(solution)/shard_map/ppermute | solution.py:295
  37.6 2.5 %collective-permute-start = (bf16[192,512]{1,0:T(8,128)(2,1)S(1)}, bf16[192,512]{1,0:T(8,128)(2,1)S(1)}, u32[]{:S(2)}, u32[]{:S(2)}) collective-permute-start(bf16[192,512]{1,0:T(8,128)(2,1)S(1)} %bitcast.16), channel_id=1, source_target_pairs={{0,8},{8,16},{16,24},{24,0},{1,9},{9,17},{17,25},{25,1},{2,10},{10... | collective-permute-start | bytes 589832 | tf_op jit(solution)/shard_map/ppermute | solution.py:295
  40.1 0.1 select_reduce_fusion.2
  40.2 3.1 %collective-permute-done.1.q2_ref = bf16[192,512]{1,0:T(8,128)(2,1)S(1)} collective-permute-done((bf16[192,512]{1,0:T(8,128)(2,1)S(1)}, bf16[192,512]{1,0:T(8,128)(2,1)S(1)}, u32[]{:S(2)}, u32[]{:S(2)}) %collective-permute-start.1) | collective-permute-done | bytes 196640 | tf_op jit(solution)/shard_map/ppermute | solution.py:295
  43.3 3.0 %collective-permute-done.q1_ref = bf16[192,512]{1,0:T(8,128)(2,1)S(1)} collective-permute-done((bf16[192,512]{1,0:T(8,128)(2,1)S(1)}, bf16[192,512]{1,0:T(8,128)(2,1)S(1)}, u32[]{:S(2)}, u32[]{:S(2)}) %collective-permute-start) | collective-permute-done | bytes 196640 | tf_op jit(solution)/shard_map/ppermute | solution.py:295
  46.3 5.1 %all-to-all-done.1 = bf16[64,24,256]{2,1,0:T(8,128)(2,1)S(1)} async-done(((bf16[64,24,256]{2,1,0:T(8,128)(2,1)}), bf16[64,24,256]{2,1,0:T(8,128)(2,1)S(1)}, u32[]{:S(2)}, u32[]{:S(2)}) %all-to-all-start.1) | async-done | bytes 786464 | tf_op jit(solution)/shard_map/all_to_all | solution.py:282
  51.5 6.5 %collective-permute-start.3 = (bf16[1536,256]{1,0:T(8,128)(2,1)S(1)}, bf16[1536,256]{1,0:T(8,128)(2,1)S(1)}, u32[]{:S(2)}, u32[]{:S(2)}) collective-permute-start(bf16[1536,256]{1,0:T(8,128)(2,1)S(1)} %bitcast.12), channel_id=1, source_target_pairs={{0,1},{1,0},{2,3},{3,2},{4,5},{5,4},{6,7},{7,6},{8,9},{9,8},{10,11... | collective-permute-start | bytes 2359304 | tf_op jit(solution)/shard_map/ppermute | solution.py:295
  58.0 0.1 add.79.columns
  58.1 0.2 convert_reduce_fusion.3
  58.3 0.1 select_reduce_fusion.4
  58.4 0.2 convert_reduce_fusion.1
  58.6 0.1 concatenate.3.scalars
  58.7 1.2 %collective-permute-done.3.other_ref = bf16[1536,256]{1,0:T(8,128)(2,1)S(1)} collective-permute-done((bf16[1536,256]{1,0:T(8,128)(2,1)S(1)}, bf16[1536,256]{1,0:T(8,128)(2,1)S(1)}, u32[]{:S(2)}, u32[]{:S(2)}) %collective-permute-start.3) | collective-permute-done | bytes 786464 | tf_op jit(solution)/shard_map/ppermute | solution.py:295
  59.8 15.3 %attend.1 = bf16[832,512]{1,0:T(8,128)(2,1)S(1)} custom-call(s32[112]{0:T(128)S(1)} %concatenate.3.scalars, s32[3,1,1024]{2,1,0:T(1,128)S(1)} %add.79.columns, bf16[192,512]{1,0:T(8,128)(2,1)S(1)} %bitcast.17, bf16[192,512]{1,0:T(8,128)(2,1)S(1)} %collective-permute-done.q1_ref, bf16[192,512]{1,0:T(8,128)(2,1)S(1)} %collective-permute-done.1.q2_ref, ...), custom_call_target="tpu_custom_call" | custom-call | flops 2400000000 | bytes 4000000 | tf_op jit(solution)/shard_map/attend/pallas_call | solution.py:221
  75.2 17.5 %all_to_all.21.parts_ref = bf16[4,208,512]{2,1,0:T(8,128)(2,1)} all-to-all(bf16[4,208,512]{2,1,0:T(8,128)(2,1)S(1)} %bitcast.11), channel_id=1, replica_groups=mesh['z2'=2,'z1'=2,'zl'=2,'yl'=2,'x'=4,'y2'=2,'y1'=2,'core'=2] {'x'}, dimensions={0} | all-to-all | bytes 1703936 | tf_op jit(solution)/shard_map/all_to_all | solution.py:282
  92.7 2.5 %combine.1 = bf16[192,512]{1,0:T(8,128)(2,1)} custom-call(bf16[4,208,512]{2,1,0:T(8,128)(2,1)} %all_to_all.21.parts_ref), custom_call_target="tpu_custom_call" | custom-call | tf_op jit(solution)/shard_map/combine/pallas_call | solution.py:272
  95.2 10.2 %all_to_all.22 = bf16[8,24,512]{2,1,0:T(8,128)(2,1)S(1)} all-to-all(bf16[8,24,512]{2,1,0:T(8,128)(2,1)} %bitcast.18), channel_id=1, replica_groups=mesh['z2'=2,'z1'=2,'zl'=2,'yl'=2,'x'=4,'y2'=2,'y1'=2,'core'=2] {'zl','yl..., dimensions={0} | all-to-all | bytes 393216 | tf_op jit(solution)/shard_map/all_to_all | solution.py:282
  105.5 0.8 reshape.159
  (15 shorter events, 0.3 us)
Async XLA Ops:
  1.1 14.2 %copy-start = (bf16[24,8,256]{2,1,0:T(8,128)(2,1)S(1)}, bf16[24,8,256]{2,1,0:T(8,128)(2,1)}, u32[]{:S(2)}) copy-start(bf16[24,8,256]{2,1,0:T(8,128)(2,1)} %param.4) | copy-start | bytes 294916
  16.3 35.2 %all-to-all-start.1 = ((bf16[64,24,256]{2,1,0:T(8,128)(2,1)}), bf16[64,24,256]{2,1,0:T(8,128)(2,1)S(1)}, u32[]{:S(2)}, u32[]{:S(2)}) async-start(bf16[64,24,256]{2,1,0:T(8,128)(2,1)} %bitcast.4), calls=%async_computation.1 | async-start | bytes 1572864 | tf_op jit(solution)/shard_map/all_to_all | solution.py:282
  29.0 0.7 copy-start.1
  30.7 9.5 %collective-permute-start.2 = (bf16[192,512]{1,0:T(8,128)(2,1)S(1)}, bf16[192,512]{1,0:T(8,128)(2,1)S(1)}, u32[]{:S(2)}, u32[]{:S(2)}) collective-permute-start(bf16[192,512]{1,0:T(8,128)(2,1)S(1)} %bitcast.14), channel_id=1, source_target_pairs={{0,24},{8,0},{16,8},{24,16},{1,25},{9,1},{17,9},{25,17},{2,26},{10... | collective-permute-start | bytes 589832 | tf_op jit(solution)/shard_map/ppermute | solution.py:295
  35.1 8.2 %collective-permute-start.1 = (bf16[192,512]{1,0:T(8,128)(2,1)S(1)}, bf16[192,512]{1,0:T(8,128)(2,1)S(1)}, u32[]{:S(2)}, u32[]{:S(2)}) collective-permute-start(bf16[192,512]{1,0:T(8,128)(2,1)S(1)} %bitcast.15), channel_id=1, source_target_pairs={{0,16},{8,24},{16,0},{24,8},{1,17},{9,25},{17,1},{25,9},{2,18},{10... | collective-permute-start | bytes 589832 | tf_op jit(solution)/shard_map/ppermute | solution.py:295
  37.6 8.8 %collective-permute-start = (bf16[192,512]{1,0:T(8,128)(2,1)S(1)}, bf16[192,512]{1,0:T(8,128)(2,1)S(1)}, u32[]{:S(2)}, u32[]{:S(2)}) collective-permute-start(bf16[192,512]{1,0:T(8,128)(2,1)S(1)} %bitcast.16), channel_id=1, source_target_pairs={{0,8},{8,16},{16,24},{24,0},{1,9},{9,17},{17,25},{25,1},{2,10},{10... | collective-permute-start | bytes 589832 | tf_op jit(solution)/shard_map/ppermute | solution.py:295
  51.5 8.4 %collective-permute-start.3 = (bf16[1536,256]{1,0:T(8,128)(2,1)S(1)}, bf16[1536,256]{1,0:T(8,128)(2,1)S(1)}, u32[]{:S(2)}, u32[]{:S(2)}) collective-permute-start(bf16[1536,256]{1,0:T(8,128)(2,1)S(1)} %bitcast.12), channel_id=1, source_target_pairs={{0,1},{1,0},{2,3},{3,2},{4,5},{5,4},{6,7},{7,6},{8,9},{9,8},{10,11... | collective-permute-start | bytes 2359304 | tf_op jit(solution)/shard_map/ppermute | solution.py:295

commit v4 on v3

--- a/solution.py
+++ b/solution.py
@@ -21,9 +21,9 @@
 Q_ROWS = Q_UNITS * UNIT
 TOGETHER = 4
 GROUP_ROWS = TOGETHER * GROUP * UNIT
-PARTS = 2
+PARTS = 4
 PART_ROWS = GROUP_ROWS // PARTS
-CHUNK = 1024
+CHUNK = 768
 CHUNKS = KEYS // CHUNK
 Q_COLS = GROUP * HEAD_DIM
 BLOCK_ROWS = 192
@@ -148,25 +148,17 @@
                     preferred_element_type=jnp.float32,
                 )
 
-        free = scalars[BELOW + first] * SPAN // CHUNK
         ends = (scalars[UPTO + first + TOGETHER - 1] * SPAN + CHUNK - 1) // CHUNK
-
-        def free_step(chunk, _):
-            score(chunk, False)
-            return 0
-
-        def masked_step(chunk, _):
-            score(chunk, True)
-            return 0
-
-        def weigh_step(chunk, _):
-            weigh(chunk)
-            return 0
-
-        lax.fori_loop(0, free, free_step, 0)
-        lax.fori_loop(free, ends, masked_step, 0)
-        top[...] = jnp.broadcast_to(jnp.max(top[...], axis=1, keepdims=True), top.shape)
-        lax.fori_loop(0, ends, weigh_step, 0)
+        for count in range(1, CHUNKS + 1):
+
+            @pl.when(ends == count)
+            def _():
+                for chunk in range(count):
+                    score(chunk, True)
+                highest = jnp.max(top[...], axis=1, keepdims=True)
+                top[...] = jnp.broadcast_to(highest, top.shape)
+                for chunk in range(count):
+                    weigh(chunk)
 
         for u in range(TOGETHER):
             unit = scalars[Q_INDEX + first + u]
@@ -274,6 +266,7 @@
         out_shape=jax.ShapeDtypeStruct((BLOCK_ROWS, Q_COLS), jnp.bfloat16),
         in_specs=[vmem],
         out_specs=vmem,
+        compiler_params=pltpu.CompilerParams(vmem_limit_bytes=8 * 1024 * 1024),
         name="combine",
     )(parts)
 

time: 107 us -> 99.2 us (0.927)
  Pallas kernels: 17.9 us -> 12.4 us
  blocking collectives: 41.9 us -> 39.4 us
    pallas_call x1, Pallas kernels: 15.3 us -> 11.7 us  [attend(): pl.pallas_call(attend_kernel, out_shape=jax.ShapeDtypeStruct((blocks * (B...]
    all_to_all x3, blocking collectives: 41.9 us -> 39.4 us  [exchange(): return lax.all_to_all(blocks, axes, split_axis=0, concat_axis=0, tiled=True)]
    pallas_call x1, Pallas kernels: 2.52 us -> 0.69 us  [combine(): pl.pallas_call(combine_kernel, out_shape=jax.ShapeDtypeStruct((BLOCK_ROWS...]
where the time goes in v4:
time: 99.2 us; the launch traced here: 98.3 us
  blocking collectives  39.4 us (40%)
  starting transfers between devices  28.5 us (29%)
  Pallas kernels  12.4 us (12%)
  waiting for transfers between devices  12.3 us (12%)
  local copies, waits for them, and re-layouts  4.26 us (4%)
  other arithmetic  1.26 us (1%)
    all_to_all x3, blocking collectives, exchange(): return lax.all_to_all(blocks, axes, split_axis=0, concat_axis=0, tiled=True)  39.4 us
    ppermute x4, starting transfers between devices, turn(): lax.ppermute(block, axis, [(i, (i + step) % size) for i in range(size)])  15.8 us
    all_to_all x1, starting transfers between devices, exchange(): return lax.all_to_all(blocks, axes, split_axis=0, concat_axis=0, tiled=True)  12.7 us
    pallas_call x1, Pallas kernels, attend(): pl.pallas_call(attend_kernel, out_shape=jax.ShapeDtypeStruct((blocks * (B...  11.7 us
    ppermute x4, waiting for transfers between devices, turn(): lax.ppermute(block, axis, [(i, (i + step) % size) for i in range(size)])  7.05 us
    all_to_all x1, waiting for transfers between devices, exchange(): return lax.all_to_all(blocks, axes, split_axis=0, concat_axis=0, tiled=True)  5.27 us
  transfers between devices with their start and end apart: 5, of which 4 were waited for; matrix products, arithmetic and copies ran while one was open for 2% of the time, Pallas kernels for 0%

profile of v4, /device:TPU:1, one launch (start us, length us, event | category | flops | bytes accessed | tf_op | source)
XLA Modules:
  0.0 98.3 jit_solution(11391797093693555899)
XLA Ops:
  0.0 1.1 %reshape.177 = bf16[24,8,512]{2,1,0:T(8,128)(2,1)S(1)} reshape(bf16[24,32,128]{2,1,0:T(8,128)(2,1)} %param.3) | data formatting | bytes 393216 | tf_op jit(solution)/shard_map/reshape | solution.py:294
  1.1 14.2 %all_to_all.20 = bf16[8,24,512]{2,1,0:T(8,128)(2,1)S(1)} all-to-all(bf16[8,24,512]{2,1,0:T(8,128)(2,1)S(1)} %bitcast.19), channel_id=1, replica_groups=mesh['z2'=2,'z1'=2,'zl'=2,'yl'=2,'x'=4,'y2'=2,'y1'=2,'core'=2] {'zl','yl..., dimensions={0} | all-to-all | bytes 393216 | tf_op jit(solution)/shard_map/all_to_all | solution.py:275
  15.3 0.9 broadcast_in_dim.125
  16.3 12.7 %all-to-all-start.1 = ((bf16[64,24,256]{2,1,0:T(8,128)(2,1)}), bf16[64,24,256]{2,1,0:T(8,128)(2,1)S(1)}, u32[]{:S(2)}, u32[]{:S(2)}) async-start(bf16[64,24,256]{2,1,0:T(8,128)(2,1)} %bitcast.4), calls=%async_computation.1 | async-start | bytes 1572864 | tf_op jit(solution)/shard_map/all_to_all | solution.py:275
  29.1 0.6 copy-done.1
  29.7 0.2 reshape.176
  29.9 0.1 broadcast_and_fusion
  30.0 0.2 select_reduce_fusion
  30.2 0.2 select_reduce_fusion.6
  30.4 0.1 lt.72
  30.5 0.1 lt.67
  30.6 4.4 %collective-permute-start.2 = (bf16[192,512]{1,0:T(8,128)(2,1)S(1)}, bf16[192,512]{1,0:T(8,128)(2,1)S(1)}, u32[]{:S(2)}, u32[]{:S(2)}) collective-permute-start(bf16[192,512]{1,0:T(8,128)(2,1)S(1)} %bitcast.15), channel_id=1, source_target_pairs={{0,24},{8,0},{16,8},{24,16},{1,25},{9,1},{17,9},{25,17},{2,26},{10... | collective-permute-start | bytes 589832 | tf_op jit(solution)/shard_map/ppermute | solution.py:288
  35.0 2.4 %collective-permute-start.1 = (bf16[192,512]{1,0:T(8,128)(2,1)S(1)}, bf16[192,512]{1,0:T(8,128)(2,1)S(1)}, u32[]{:S(2)}, u32[]{:S(2)}) collective-permute-start(bf16[192,512]{1,0:T(8,128)(2,1)S(1)} %bitcast.16), channel_id=1, source_target_pairs={{0,16},{8,24},{16,0},{24,8},{1,17},{9,25},{17,1},{25,9},{2,18},{10... | collective-permute-start | bytes 589832 | tf_op jit(solution)/shard_map/ppermute | solution.py:288
  37.4 2.5 %collective-permute-start = (bf16[192,512]{1,0:T(8,128)(2,1)S(1)}, bf16[192,512]{1,0:T(8,128)(2,1)S(1)}, u32[]{:S(2)}, u32[]{:S(2)}) collective-permute-start(bf16[192,512]{1,0:T(8,128)(2,1)S(1)} %bitcast.17), channel_id=1, source_target_pairs={{0,8},{8,16},{16,24},{24,0},{1,9},{9,17},{17,25},{25,1},{2,10},{10... | collective-permute-start | bytes 589832 | tf_op jit(solution)/shard_map/ppermute | solution.py:288
  39.9 0.2 convert_reduce_fusion
  40.1 0.1 select_reduce_fusion.2
  40.2 3.0 %collective-permute-done.1.q2_ref = bf16[192,512]{1,0:T(8,128)(2,1)S(1)} collective-permute-done((bf16[192,512]{1,0:T(8,128)(2,1)S(1)}, bf16[192,512]{1,0:T(8,128)(2,1)S(1)}, u32[]{:S(2)}, u32[]{:S(2)}) %collective-permute-start.1) | collective-permute-done | bytes 196640 | tf_op jit(solution)/shard_map/ppermute | solution.py:288
  43.2 3.0 %collective-permute-done.q1_ref = bf16[192,512]{1,0:T(8,128)(2,1)S(1)} collective-permute-done((bf16[192,512]{1,0:T(8,128)(2,1)S(1)}, bf16[192,512]{1,0:T(8,128)(2,1)S(1)}, u32[]{:S(2)}, u32[]{:S(2)}) %collective-permute-start) | collective-permute-done | bytes 196640 | tf_op jit(solution)/shard_map/ppermute | solution.py:288
  46.2 5.3 %all-to-all-done.1 = bf16[64,24,256]{2,1,0:T(8,128)(2,1)S(1)} async-done(((bf16[64,24,256]{2,1,0:T(8,128)(2,1)}), bf16[64,24,256]{2,1,0:T(8,128)(2,1)S(1)}, u32[]{:S(2)}, u32[]{:S(2)}) %all-to-all-start.1) | async-done | bytes 786464 | tf_op jit(solution)/shard_map/all_to_all | solution.py:275
  51.5 6.5 %collective-permute-start.3 = (bf16[1536,256]{1,0:T(8,128)(2,1)S(1)}, bf16[1536,256]{1,0:T(8,128)(2,1)S(1)}, u32[]{:S(2)}, u32[]{:S(2)}) collective-permute-start(bf16[1536,256]{1,0:T(8,128)(2,1)S(1)} %bitcast.13), channel_id=1, source_target_pairs={{0,1},{1,0},{2,3},{3,2},{4,5},{5,4},{6,7},{7,6},{8,9},{9,8},{10,11... | collective-permute-start | bytes 2359304 | tf_op jit(solution)/shard_map/ppermute | solution.py:288
  57.9 0.1 mul.38
  58.1 0.1 add.77
  58.2 0.2 convert_reduce_fusion.3
  58.4 0.1 select_reduce_fusion.4
  58.5 0.2 convert_reduce_fusion.1
  58.7 0.1 concatenate.3.scalars
  58.8 1.1 %collective-permute-done.3.other_ref = bf16[1536,256]{1,0:T(8,128)(2,1)S(1)} collective-permute-done((bf16[1536,256]{1,0:T(8,128)(2,1)S(1)}, bf16[1536,256]{1,0:T(8,128)(2,1)S(1)}, u32[]{:S(2)}, u32[]{:S(2)}) %collective-permute-start.3) | collective-permute-done | bytes 786464 | tf_op jit(solution)/shard_map/ppermute | solution.py:288
  59.8 11.7 %attend.1 = bf16[832,512]{1,0:T(8,128)(2,1)S(1)} custom-call(s32[112]{0:T(128)S(1)} %concatenate.3.scalars, s32[4,1,768]{2,1,0:T(1,128)S(1)} %broadcast_add_fusion.columns, bf16[192,512]{1,0:T(8,128)(2,1)S(1)} %bitcast.18, bf16[192,512]{1,0:T(8,128)(2,1)S(1)} %collective-permute-done.q1_ref, bf16[192,512]{1,0:T(8,128)(2,1)S(1)} %collective-permute-done.1.q2_ref, ...), custom_call_target="tpu_custom_call" | custom-call | flops 2400000000 | bytes 4000000 | tf_op jit(solution)/shard_map/attend/pallas_call | solution.py:213
  71.5 16.0 %all_to_all.21.parts_ref = bf16[4,208,512]{2,1,0:T(8,128)(2,1)S(1)} all-to-all(bf16[4,208,512]{2,1,0:T(8,128)(2,1)S(1)} %bitcast.11), channel_id=1, replica_groups=mesh['z2'=2,'z1'=2,'zl'=2,'yl'=2,'x'=4,'y2'=2,'y1'=2,'core'=2] {'x'}, dimensions={0} | all-to-all | bytes 1703936 | tf_op jit(solution)/shard_map/all_to_all | solution.py:275
  87.5 0.7 combine.1
  88.2 9.3 %all_to_all.22 = bf16[8,24,512]{2,1,0:T(8,128)(2,1)S(1)} all-to-all(bf16[8,24,512]{2,1,0:T(8,128)(2,1)S(1)} %bitcast.12), channel_id=1, replica_groups=mesh['z2'=2,'z1'=2,'zl'=2,'yl'=2,'x'=4,'y2'=2,'y1'=2,'core'=2] {'zl','yl..., dimensions={0} | all-to-all | bytes 393216 | tf_op jit(solution)/shard_map/all_to_all | solution.py:275
  97.5 0.8 reshape.183
  (19 shorter events, 0.4 us)
Async XLA Ops:
  1.1 14.2 %copy-start = (bf16[24,8,256]{2,1,0:T(8,128)(2,1)S(1)}, bf16[24,8,256]{2,1,0:T(8,128)(2,1)}, u32[]{:S(2)}) copy-start(bf16[24,8,256]{2,1,0:T(8,128)(2,1)} %param.4) | copy-start | bytes 294916
  16.3 35.2 %all-to-all-start.1 = ((bf16[64,24,256]{2,1,0:T(8,128)(2,1)}), bf16[64,24,256]{2,1,0:T(8,128)(2,1)S(1)}, u32[]{:S(2)}, u32[]{:S(2)}) async-start(bf16[64,24,256]{2,1,0:T(8,128)(2,1)} %bitcast.4), calls=%async_computation.1 | async-start | bytes 1572864 | tf_op jit(solution)/shard_map/all_to_all | solution.py:275
  29.0 0.7 copy-start.1
  30.6 9.6 %collective-permute-start.2 = (bf16[192,512]{1,0:T(8,128)(2,1)S(1)}, bf16[192,512]{1,0:T(8,128)(2,1)S(1)}, u32[]{:S(2)}, u32[]{:S(2)}) collective-permute-start(bf16[192,512]{1,0:T(8,128)(2,1)S(1)} %bitcast.15), channel_id=1, source_target_pairs={{0,24},{8,0},{16,8},{24,16},{1,25},{9,1},{17,9},{25,17},{2,26},{10... | collective-permute-start | bytes 589832 | tf_op jit(solution)/shard_map/ppermute | solution.py:288
  35.0 8.2 %collective-permute-start.1 = (bf16[192,512]{1,0:T(8,128)(2,1)S(1)}, bf16[192,512]{1,0:T(8,128)(2,1)S(1)}, u32[]{:S(2)}, u32[]{:S(2)}) collective-permute-start(bf16[192,512]{1,0:T(8,128)(2,1)S(1)} %bitcast.16), channel_id=1, source_target_pairs={{0,16},{8,24},{16,0},{24,8},{1,17},{9,25},{17,1},{25,9},{2,18},{10... | collective-permute-start | bytes 589832 | tf_op jit(solution)/shard_map/ppermute | solution.py:288
  37.4 8.8 %collective-permute-start = (bf16[192,512]{1,0:T(8,128)(2,1)S(1)}, bf16[192,512]{1,0:T(8,128)(2,1)S(1)}, u32[]{:S(2)}, u32[]{:S(2)}) collective-permute-start(bf16[192,512]{1,0:T(8,128)(2,1)S(1)} %bitcast.17), channel_id=1, source_target_pairs={{0,8},{8,16},{16,24},{24,0},{1,9},{9,17},{17,25},{25,1},{2,10},{10... | collective-permute-start | bytes 589832 | tf_op jit(solution)/shard_map/ppermute | solution.py:288
  51.5 8.4 %collective-permute-start.3 = (bf16[1536,256]{1,0:T(8,128)(2,1)S(1)}, bf16[1536,256]{1,0:T(8,128)(2,1)S(1)}, u32[]{:S(2)}, u32[]{:S(2)}) collective-permute-start(bf16[1536,256]{1,0:T(8,128)(2,1)S(1)} %bitcast.13), channel_id=1, source_target_pairs={{0,1},{1,0},{2,3},{3,2},{4,5},{5,4},{6,7},{7,6},{8,9},{9,8},{10,11... | collective-permute-start | bytes 2359304 | tf_op jit(solution)/shard_map/ppermute | solution.py:288

commit v5 on v4

--- a/solution.py
+++ b/solution.py
@@ -111,10 +111,8 @@
                     pl.ds(source, UNIT), g * HEAD_DIM : (g + 1) * HEAD_DIM
                 ]
                 q_position[to, :] = position
-        top[...] = jnp.full(top.shape, LOWEST, jnp.float32)
-        total[...] = jnp.zeros(total.shape, jnp.float32)
-
-        def score(chunk, masked):
+
+        def score(chunk, masked, first_chunk):
             for rows in part_rows:
                 block = jnp.dot(
                     q_group[rows, :], keys_t[chunk], preferred_element_type=jnp.float32
@@ -133,39 +131,48 @@
                 else:
                     tiles = [block[:, t : t + HEAD_DIM] for t in range(0, CHUNK, HEAD_DIM)]
                 scores[chunk, rows, :] = block
-                top[rows, :] = functools.reduce(jnp.maximum, tiles, top[rows, :])
-
-        def weigh(chunk):
+                if not first_chunk:
+                    tiles.append(top[rows, :])
+                top[rows, :] = functools.reduce(jnp.maximum, tiles)
+
+        def weigh(chunk, first_chunk):
             for rows in part_rows:
                 highest = top[rows, :]
                 tiles = [
                     jnp.exp2((scores[chunk, rows, t : t + HEAD_DIM] - highest) * EXPONENT)
                     for t in range(0, CHUNK, HEAD_DIM)
                 ]
-                total[rows, :] += jnp.dot(
+                product = jnp.dot(
                     jnp.concatenate(tiles, axis=1).astype(jnp.bfloat16),
                     values[chunk],
                     preferred_element_type=jnp.float32,
                 )
+                total[rows, :] = product if first_chunk else total[rows, :] + product
 
         ends = (scalars[UPTO + first + TOGETHER - 1] * SPAN + CHUNK - 1) // CHUNK
+        @pl.when(ends == 0)
+        def _():
+            top[...] = jnp.full(top.shape, LOWEST, jnp.float32)
+            total[...] = jnp.zeros(total.shape, jnp.float32)
+
         for count in range(1, CHUNKS + 1):
 
             @pl.when(ends == count)
             def _():
                 for chunk in range(count):
-                    score(chunk, True)
+                    score(chunk, True, chunk == 0)
                 highest = jnp.max(top[...], axis=1, keepdims=True)
                 top[...] = jnp.broadcast_to(highest, top.shape)
                 for chunk in range(count):
-                    weigh(chunk)
+                    weigh(chunk, chunk == 0)
 
         for u in range(TOGETHER):
             unit = scalars[Q_INDEX + first + u]
             block, within = (scalars[HERE] - unit // 4) % 4, unit % 4
             target = block * (BLOCK_ROWS + STAT_ROWS) + within * UNIT
             target = pl.ds(pl.multiple_of(target, 16), UNIT)
-            packed = jnp.zeros((UNIT, HEAD_DIM), jnp.float32)
+            tops = jnp.full((UNIT, HEAD_DIM), LOWEST, jnp.float32)
+            sums = jnp.ones((UNIT, HEAD_DIM), jnp.float32)
             for g in range(GROUP):
                 part = slice((u * GROUP + g) * UNIT, (u * GROUP + g + 1) * UNIT)
                 weight_sum = total[part, HEAD_DIM:]
@@ -175,14 +182,15 @@
                 out_ref[target, g * HEAD_DIM : (g + 1) * HEAD_DIM] = (
                     total[part, :HEAD_DIM] / safe
                 ).astype(jnp.bfloat16)
-                level = jnp.where(some, highest * EXPONENT + jnp.log2(safe), LOWEST)
-                high = level.astype(jnp.bfloat16).astype(jnp.float32)
-                rest = level - high
-                middle = rest.astype(jnp.bfloat16).astype(jnp.float32)
-                low = rest - middle
-                packed = jnp.where(lane == 3 * g, high, packed)
-                packed = jnp.where(lane == 3 * g + 1, middle, packed)
-                packed = jnp.where(lane == 3 * g + 2, low, packed)
+                here = (lane // 3 == g) & some
+                tops = jnp.where(here, highest, tops)
+                sums = jnp.where(here, safe, sums)
+            level = jnp.where(tops > LOWEST, tops * EXPONENT + jnp.log2(sums), LOWEST)
+            high = level.astype(jnp.bfloat16).astype(jnp.float32)
+            rest = level - high
+            middle = rest.astype(jnp.bfloat16).astype(jnp.float32)
+            packed = jnp.where(lane % 3 == 1, middle, rest - middle)
+            packed = jnp.where(lane % 3 == 0, high, packed)
             target = pl.ds(pl.multiple_of(block * BLOCK_ROWS + within * UNIT, UNIT), UNIT)
             stats[target, :] = packed.astype(jnp.bfloat16)
         return 0

time: 99.2 us -> 98.9 us (level)
  no operation moved by 1% of the time
where the time goes in v5:
time: 98.9 us; the launch traced here: 97.4 us
  blocking collectives  38.5 us (39%)
  starting transfers between devices  28.5 us (29%)
  Pallas kernels  12.4 us (13%)
  waiting for transfers between devices  12.3 us (12%)
  local copies, waits for them, and re-layouts  4.26 us (4%)
  other arithmetic  1.26 us (1%)
    all_to_all x3, blocking collectives, exchange(): return lax.all_to_all(blocks, axes, split_axis=0, concat_axis=0, tiled=True)  38.5 us
    ppermute x4, starting transfers between devices, turn(): lax.ppermute(block, axis, [(i, (i + step) % size) for i in range(size)])  15.8 us
    all_to_all x1, starting transfers between devices, exchange(): return lax.all_to_all(blocks, axes, split_axis=0, concat_axis=0, tiled=True)  12.7 us
    pallas_call x1, Pallas kernels, attend(): pl.pallas_call(attend_kernel, out_shape=jax.ShapeDtypeStruct((blocks * (B...  11.7 us
    ppermute x4, waiting for transfers between devices, turn(): lax.ppermute(block, axis, [(i, (i + step) % size) for i in range(size)])  7.05 us
    all_to_all x1, waiting for transfers between devices, exchange(): return lax.all_to_all(blocks, axes, split_axis=0, concat_axis=0, tiled=True)  5.27 us
  transfers between devices with their start and end apart: 5, of which 4 were waited for; matrix products, arithmetic and copies ran while one was open for 2% of the time, Pallas kernels for 0%

profile of v5, /device:TPU:1, one launch (start us, length us, event | category | flops | bytes accessed | tf_op | source)
XLA Modules:
  0.0 97.4 jit_solution(15157344469651867530)
XLA Ops:
  0.0 1.1 %reshape.177 = bf16[24,8,512]{2,1,0:T(8,128)(2,1)S(1)} reshape(bf16[24,32,128]{2,1,0:T(8,128)(2,1)} %param.3) | data formatting | bytes 393216 | tf_op jit(solution)/shard_map/reshape | solution.py:302
  1.1 14.2 %all_to_all.20 = bf16[8,24,512]{2,1,0:T(8,128)(2,1)S(1)} all-to-all(bf16[8,24,512]{2,1,0:T(8,128)(2,1)S(1)} %bitcast.19), channel_id=1, replica_groups=mesh['z2'=2,'z1'=2,'zl'=2,'yl'=2,'x'=4,'y2'=2,'y1'=2,'core'=2] {'zl','yl..., dimensions={0} | all-to-all | bytes 393216 | tf_op jit(solution)/shard_map/all_to_all | solution.py:283
  15.3 0.9 broadcast_in_dim.125
  16.3 12.7 %all-to-all-start.1 = ((bf16[64,24,256]{2,1,0:T(8,128)(2,1)}), bf16[64,24,256]{2,1,0:T(8,128)(2,1)S(1)}, u32[]{:S(2)}, u32[]{:S(2)}) async-start(bf16[64,24,256]{2,1,0:T(8,128)(2,1)} %bitcast.4), calls=%async_computation.1 | async-start | bytes 1572864 | tf_op jit(solution)/shard_map/all_to_all | solution.py:283
  29.1 0.6 copy-done.1
  29.7 0.2 reshape.176
  29.9 0.1 broadcast_and_fusion
  30.0 0.2 select_reduce_fusion
  30.2 0.2 select_reduce_fusion.6
  30.4 0.1 lt.72
  30.5 0.1 lt.67
  30.6 4.4 %collective-permute-start.2 = (bf16[192,512]{1,0:T(8,128)(2,1)S(1)}, bf16[192,512]{1,0:T(8,128)(2,1)S(1)}, u32[]{:S(2)}, u32[]{:S(2)}) collective-permute-start(bf16[192,512]{1,0:T(8,128)(2,1)S(1)} %bitcast.15), channel_id=1, source_target_pairs={{0,24},{8,0},{16,8},{24,16},{1,25},{9,1},{17,9},{25,17},{2,26},{10... | collective-permute-start | bytes 589832 | tf_op jit(solution)/shard_map/ppermute | solution.py:296
  35.0 2.4 %collective-permute-start.1 = (bf16[192,512]{1,0:T(8,128)(2,1)S(1)}, bf16[192,512]{1,0:T(8,128)(2,1)S(1)}, u32[]{:S(2)}, u32[]{:S(2)}) collective-permute-start(bf16[192,512]{1,0:T(8,128)(2,1)S(1)} %bitcast.16), channel_id=1, source_target_pairs={{0,16},{8,24},{16,0},{24,8},{1,17},{9,25},{17,1},{25,9},{2,18},{10... | collective-permute-start | bytes 589832 | tf_op jit(solution)/shard_map/ppermute | solution.py:296
  37.4 2.5 %collective-permute-start = (bf16[192,512]{1,0:T(8,128)(2,1)S(1)}, bf16[192,512]{1,0:T(8,128)(2,1)S(1)}, u32[]{:S(2)}, u32[]{:S(2)}) collective-permute-start(bf16[192,512]{1,0:T(8,128)(2,1)S(1)} %bitcast.17), channel_id=1, source_target_pairs={{0,8},{8,16},{16,24},{24,0},{1,9},{9,17},{17,25},{25,1},{2,10},{10... | collective-permute-start | bytes 589832 | tf_op jit(solution)/shard_map/ppermute | solution.py:296
  39.9 0.2 convert_reduce_fusion
  40.1 0.1 select_reduce_fusion.2
  40.2 3.0 %collective-permute-done.1.q2_ref = bf16[192,512]{1,0:T(8,128)(2,1)S(1)} collective-permute-done((bf16[192,512]{1,0:T(8,128)(2,1)S(1)}, bf16[192,512]{1,0:T(8,128)(2,1)S(1)}, u32[]{:S(2)}, u32[]{:S(2)}) %collective-permute-start.1) | collective-permute-done | bytes 196640 | tf_op jit(solution)/shard_map/ppermute | solution.py:296
  43.2 3.0 %collective-permute-done.q1_ref = bf16[192,512]{1,0:T(8,128)(2,1)S(1)} collective-permute-done((bf16[192,512]{1,0:T(8,128)(2,1)S(1)}, bf16[192,512]{1,0:T(8,128)(2,1)S(1)}, u32[]{:S(2)}, u32[]{:S(2)}) %collective-permute-start) | collective-permute-done | bytes 196640 | tf_op jit(solution)/shard_map/ppermute | solution.py:296
  46.2 5.3 %all-to-all-done.1 = bf16[64,24,256]{2,1,0:T(8,128)(2,1)S(1)} async-done(((bf16[64,24,256]{2,1,0:T(8,128)(2,1)}), bf16[64,24,256]{2,1,0:T(8,128)(2,1)S(1)}, u32[]{:S(2)}, u32[]{:S(2)}) %all-to-all-start.1) | async-done | bytes 786464 | tf_op jit(solution)/shard_map/all_to_all | solution.py:283
  51.5 6.5 %collective-permute-start.3 = (bf16[1536,256]{1,0:T(8,128)(2,1)S(1)}, bf16[1536,256]{1,0:T(8,128)(2,1)S(1)}, u32[]{:S(2)}, u32[]{:S(2)}) collective-permute-start(bf16[1536,256]{1,0:T(8,128)(2,1)S(1)} %bitcast.13), channel_id=1, source_target_pairs={{0,1},{1,0},{2,3},{3,2},{4,5},{5,4},{6,7},{7,6},{8,9},{9,8},{10,11... | collective-permute-start | bytes 2359304 | tf_op jit(solution)/shard_map/ppermute | solution.py:296
  57.9 0.1 mul.38
  58.1 0.1 add.77
  58.2 0.2 convert_reduce_fusion.3
  58.4 0.1 select_reduce_fusion.4
  58.5 0.2 convert_reduce_fusion.1
  58.7 0.1 concatenate.3.scalars
  58.8 1.1 %collective-permute-done.3.other_ref = bf16[1536,256]{1,0:T(8,128)(2,1)S(1)} collective-permute-done((bf16[1536,256]{1,0:T(8,128)(2,1)S(1)}, bf16[1536,256]{1,0:T(8,128)(2,1)S(1)}, u32[]{:S(2)}, u32[]{:S(2)}) %collective-permute-start.3) | collective-permute-done | bytes 786464 | tf_op jit(solution)/shard_map/ppermute | solution.py:296
  59.8 11.7 %attend.1 = bf16[832,512]{1,0:T(8,128)(2,1)S(1)} custom-call(s32[112]{0:T(128)S(1)} %concatenate.3.scalars, s32[4,1,768]{2,1,0:T(1,128)S(1)} %broadcast_add_fusion.columns, bf16[192,512]{1,0:T(8,128)(2,1)S(1)} %bitcast.18, bf16[192,512]{1,0:T(8,128)(2,1)S(1)} %collective-permute-done.q1_ref, bf16[192,512]{1,0:T(8,128)(2,1)S(1)} %collective-permute-done.1.q2_ref, ...), custom_call_target="tpu_custom_call" | custom-call | flops 2400000000 | bytes 4000000 | tf_op jit(solution)/shard_map/attend/pallas_call | solution.py:221
  71.6 15.0 %all_to_all.21.parts_ref = bf16[4,208,512]{2,1,0:T(8,128)(2,1)S(1)} all-to-all(bf16[4,208,512]{2,1,0:T(8,128)(2,1)S(1)} %bitcast.11), channel_id=1, replica_groups=mesh['z2'=2,'z1'=2,'zl'=2,'yl'=2,'x'=4,'y2'=2,'y1'=2,'core'=2] {'x'}, dimensions={0} | all-to-all | bytes 1703936 | tf_op jit(solution)/shard_map/all_to_all | solution.py:283
  86.6 0.7 combine.1
  87.3 9.3 %all_to_all.22 = bf16[8,24,512]{2,1,0:T(8,128)(2,1)S(1)} all-to-all(bf16[8,24,512]{2,1,0:T(8,128)(2,1)S(1)} %bitcast.12), channel_id=1, replica_groups=mesh['z2'=2,'z1'=2,'zl'=2,'yl'=2,'x'=4,'y2'=2,'y1'=2,'core'=2] {'zl','yl..., dimensions={0} | all-to-all | bytes 393216 | tf_op jit(solution)/shard_map/all_to_all | solution.py:283
  96.6 0.8 reshape.183
  (19 shorter events, 0.4 us)
Async XLA Ops:
  1.1 14.2 %copy-start = (bf16[24,8,256]{2,1,0:T(8,128)(2,1)S(1)}, bf16[24,8,256]{2,1,0:T(8,128)(2,1)}, u32[]{:S(2)}) copy-start(bf16[24,8,256]{2,1,0:T(8,128)(2,1)} %param.4) | copy-start | bytes 294916
  16.3 35.2 %all-to-all-start.1 = ((bf16[64,24,256]{2,1,0:T(8,128)(2,1)}), bf16[64,24,256]{2,1,0:T(8,128)(2,1)S(1)}, u32[]{:S(2)}, u32[]{:S(2)}) async-start(bf16[64,24,256]{2,1,0:T(8,128)(2,1)} %bitcast.4), calls=%async_computation.1 | async-start | bytes 1572864 | tf_op jit(solution)/shard_map/all_to_all | solution.py:283
  29.0 0.7 copy-start.1
  30.6 9.6 %collective-permute-start.2 = (bf16[192,512]{1,0:T(8,128)(2,1)S(1)}, bf16[192,512]{1,0:T(8,128)(2,1)S(1)}, u32[]{:S(2)}, u32[]{:S(2)}) collective-permute-start(bf16[192,512]{1,0:T(8,128)(2,1)S(1)} %bitcast.15), channel_id=1, source_target_pairs={{0,24},{8,0},{16,8},{24,16},{1,25},{9,1},{17,9},{25,17},{2,26},{10... | collective-permute-start | bytes 589832 | tf_op jit(solution)/shard_map/ppermute | solution.py:296
  35.0 8.2 %collective-permute-start.1 = (bf16[192,512]{1,0:T(8,128)(2,1)S(1)}, bf16[192,512]{1,0:T(8,128)(2,1)S(1)}, u32[]{:S(2)}, u32[]{:S(2)}) collective-permute-start(bf16[192,512]{1,0:T(8,128)(2,1)S(1)} %bitcast.16), channel_id=1, source_target_pairs={{0,16},{8,24},{16,0},{24,8},{1,17},{9,25},{17,1},{25,9},{2,18},{10... | collective-permute-start | bytes 589832 | tf_op jit(solution)/shard_map/ppermute | solution.py:296
  37.4 8.8 %collective-permute-start = (bf16[192,512]{1,0:T(8,128)(2,1)S(1)}, bf16[192,512]{1,0:T(8,128)(2,1)S(1)}, u32[]{:S(2)}, u32[]{:S(2)}) collective-permute-start(bf16[192,512]{1,0:T(8,128)(2,1)S(1)} %bitcast.17), channel_id=1, source_target_pairs={{0,8},{8,16},{16,24},{24,0},{1,9},{9,17},{17,25},{25,1},{2,10},{10... | collective-permute-start | bytes 589832 | tf_op jit(solution)/shard_map/ppermute | solution.py:296
  51.5 8.4 %collective-permute-start.3 = (bf16[1536,256]{1,0:T(8,128)(2,1)S(1)}, bf16[1536,256]{1,0:T(8,128)(2,1)S(1)}, u32[]{:S(2)}, u32[]{:S(2)}) collective-permute-start(bf16[1536,256]{1,0:T(8,128)(2,1)S(1)} %bitcast.13), channel_id=1, source_target_pairs={{0,1},{1,0},{2,3},{3,2},{4,5},{5,4},{6,7},{7,6},{8,9},{9,8},{10,11... | collective-permute-start | bytes 2359304 | tf_op jit(solution)/shard_map/ppermute | solution.py:296
